TPU v7x, 256 devices: a whole 4x4x8 slice. The times are simulated.
256 devices in a mesh: grp: 16 (over z, x_lo), shard: 16 (over y, x_hi, core).
Axes of the slice: x: 4 (x_hi: 2, x_lo: 2; x = x_hi * 2 + x_lo), y: 4, z: 8, core: 2. Of those that a mesh axis runs over, the one named last changes fastest.
Arguments:
- pooled: bfloat16 [6144, 256, 128], P('grp', 'shard'), may hold values from -6 to 6
- row_scale: float32 [6144, 256], P('grp', 'shard'), may hold values from 0.3 to 3
- row_ids: int32 [6144, 256], P('grp', 'shard'), may hold values from 0 to 255
- feature_order: int32 [256], replicated, may hold values from 0 to 255, each once
- compress_w: bfloat16 [2, 256, 128], replicated, may hold values from -0.375 to 0.375
- expand_w: bfloat16 [2, 128, 128], replicated, may hold values from -0.5 to 0.5
- norm_gain: float32 [2, 128], replicated, may hold values from 0.5 to 1.5
- out_grad: bfloat16 [6144, 256, 128], P(('grp', 'shard')), may hold values from -6 to 6
Outputs:
- features_out: bfloat16 [6144, 256, 128], P(('grp', 'shard'))
- table_grad: float32 [256, 256, 128], P('shard')
- compress_grad: float32 [2, 256, 128], replicated
- expand_grad: float32 [2, 128, 128], replicated
- gain_grad: float32 [2, 128], replicated
Inputs may be any that keep to these rules, and one draw needn't show every extreme that they name: `feature_order`: a permutation of 0 .. 255.
All inputs are finite; a program needn't handle non-finite values.
Results may differ from a plain program's by a relative error of at most 0.03.
Values may be sent and summed in bfloat16 or wider, within the bound.
No kernel may reach another device: no remote copies, remote signals or barrier semaphores. Data moves between devices by JAX's collectives and lax.ppermute only.
A program may use at most 128 MiB of HBM per device.

v0:
```python
import jax
import jax.numpy as jnp
from jax import lax
from jax.sharding import PartitionSpec as P

R = 256


def layers(x, wcol, expand_w, norm_gain):
    depth = wcol.shape[0]
    width = x.shape[2]
    for layer in range(depth):
        u_mat = jnp.einsum(
            "bfd,fk->bdk", x, wcol[layer], preferred_element_type=jnp.float32
        ).astype(jnp.bfloat16)
        inter = (
            jnp.einsum("bfd,bdk->bfk", x, u_mat, preferred_element_type=jnp.float32)
            / jnp.sqrt(jnp.float32(width))
        ).astype(jnp.bfloat16)
        mixed = x.astype(jnp.float32) + jnp.einsum(
            "bfk,kd->bfd", inter, expand_w[layer], preferred_element_type=jnp.float32
        )
        scale = lax.rsqrt(jnp.mean(mixed * mixed, axis=-1, keepdims=True) + 1e-06)
        x = (mixed * scale * norm_gain[layer]).astype(jnp.bfloat16)
    return x


def on_device(pooled, row_scale, row_ids, feature_order, compress_w, expand_w, norm_gain, out_grad):
    depth = compress_w.shape[0]
    features = compress_w.shape[1]
    width_k = compress_w.shape[2]
    wcol = jnp.take(compress_w, feature_order, axis=1)
    scaled = (pooled.astype(jnp.float32) * row_scale[:, :, None]).astype(jnp.bfloat16)
    x_zero = lax.all_to_all(scaled, "shard", split_axis=0, concat_axis=1, tiled=True)
    features_out, pull = jax.vjp(layers, x_zero, wcol, expand_w, norm_gain)
    grad_x, grad_w, grad_v, grad_g = pull(out_grad)
    compress_part = (
        jnp.zeros((depth, features, width_k), jnp.float32)
        .at[:, feature_order, :]
        .set(grad_w.astype(jnp.float32))
    )
    expand_part = grad_v.astype(jnp.float32)
    onehot = (row_ids[:, :, None] == jnp.arange(R, dtype=jnp.int32)[None, None, :]).astype(
        jnp.bfloat16
    )
    values = (
        lax.all_to_all(grad_x, "shard", split_axis=1, concat_axis=0, tiled=True).astype(jnp.float32)
        * row_scale[:, :, None]
    )
    high_part = values.astype(jnp.bfloat16)
    low_part = (values - high_part.astype(jnp.float32)).astype(jnp.bfloat16)
    first = jnp.einsum("bfr,bfd->frd", onehot, high_part, preferred_element_type=jnp.float32)
    second = jnp.einsum("bfr,bfd->frd", onehot, low_part, preferred_element_type=jnp.float32)
    table_part = first + second
    compress_grad, expand_grad, gain_grad = lax.psum(
        (compress_part, expand_part, grad_g), ("grp", "shard")
    )
    table_grad = lax.psum(table_part.astype(jnp.bfloat16), "grp").astype(jnp.float32)
    return (features_out, table_grad, compress_grad, expand_grad, gain_grad)


def solution(mesh):
    return jax.shard_map(
        on_device,
        mesh=mesh,
        in_specs=(
            P("grp", "shard", None),
            P("grp", "shard"),
            P("grp", "shard"),
            P(),
            P(),
            P(),
            P(),
            P(("grp", "shard"), None, None),
        ),
        out_specs=(P(("grp", "shard"), None, None), P("shard", None, None), P(), P(), P()),
        check_vma=False,
    )
```

profile of v0, /device:TPU:2, one launch (start us, length us, event | category | flops | bytes accessed | tf_op | source)
XLA Modules:
  0.0 503.5 jit_solution(16113783618436573812)
XLA Ops:
  7.2 0.0 copy-start
  7.2 0.9 copy.90
  8.1 3.0 multiply_convert_fusion.4
  11.2 6.3 %all-to-all-start = ((bf16[384,16,128]{2,1,0:T(8,128)(2,1)}), bf16[384,16,128]{2,1,0:T(8,128)(2,1)S(1)}, u32[]{:S(2)}, u32[]{:S(2)}) async-start(bf16[384,16,128]{2,1,0:T(8,128)(2,1)} %multiply_convert_fusion.4), calls=%async_computation | async-start | bytes 3145728 | tf_op jit(solution)/shard_map/all_to_all | solution.py:34
  17.4 2.6 copy.97
  20.0 1.3 gather_fusion
  21.4 0.1 select_bitcast_fusion
  21.5 19.7 %all-to-all-done = bf16[384,16,128]{2,1,0:T(8,128)(2,1)S(1)} async-done(((bf16[384,16,128]{2,1,0:T(8,128)(2,1)}), bf16[384,16,128]{2,1,0:T(8,128)(2,1)S(1)}, u32[]{:S(2)}, u32[]{:S(2)}) %all-to-all-start) | async-done | bytes 1572896 | tf_op jit(solution)/shard_map/all_to_all | solution.py:34
  41.2 0.4 copy.91
  41.6 1.7 copy.92
  43.4 0.6 convolution_convert_fusion.5
  44.0 0.6 multiply_convert_fusion.3
  44.6 0.2 copy-done.14
  44.8 0.7 multiply_reduce_fusion.1
  45.5 0.4 copy-done.8
  46.0 0.7 multiply_convert_fusion.2
  46.7 0.6 convolution_convert_fusion.4
  47.3 0.7 multiply_convert_fusion.1
  48.0 0.0 copy-start.5
  48.0 0.7 multiply_reduce_fusion
  48.7 0.4 copy-done.10
  49.1 0.8 copy-done.5
  49.9 2.9 fusion.8
  52.9 1.2 convolution_convert_fusion.3
  54.1 0.6 fusion.25
  54.7 0.9 copy-done.11
  55.6 0.6 convolution_convert_fusion.2
  56.2 2.9 fusion.9
  59.2 1.2 convolution_convert_fusion.1
  60.4 0.7 copy-done.2
  61.1 0.8 fusion.26
  62.0 0.9 copy-done.12
  62.9 0.6 convolution_convert_fusion
  63.5 2.7 bitcast_add_fusion
  66.2 2.8 copy.105
  68.9 4.4 all-to-all-start.1
  73.3 0.0 all-reduce.12.cloned.1.call-start
  73.4 2.2 fusion.30
  75.6 2.2 fusion.29
  77.8 0.9 copy.111
  78.7 0.1 broadcast_in_dim.51
  78.8 15.7 %scatter_fusion = f32[2,256,128]{2,0,1:T(2,128)S(1)} fusion(f32[2,256,128]{2,0,1:T(2,128)S(1)} %broadcast_in_dim.51, s32[256]{0:T(256)S(1)} %compare_select_fusion, f32[256,2,128]{2,1,0:T(2,128)} %copy.111), kind=kCustom, calls=%fused_computation.1 | custom fusion | bytes 787456 | tf_op jit(solution)/shard_map/scatter | solution.py:40
  94.5 0.0 copy-start.15
  94.5 0.0 copy-start.22
  94.5 4.1 fusion.34
  98.7 1.2 fusion.33
  99.8 0.7 add_convert_fusion.1
  100.5 0.0 all-reduce.12.cloned.1.call-update
  100.5 0.0 all-reduce.10.cloned.1.call-start
  100.6 1.7 copy.106
  102.3 0.4 convert_bitcast_fusion
  102.7 0.3 copy.107
  103.1 0.6 copy-done.17
  103.6 1.0 fusion.16
  104.6 1.4 fusion
  106.1 2.6 add_convert_fusion
  108.7 0.0 all-reduce.10.cloned.1.call-update
  108.7 1.6 copy.116
  110.3 80.8 %psum.31 = f32[2,128]{1,0:T(2,128)} all-reduce(f32[2,128]{1,0:T(2,128)S(1)} %pad_add_fusion), channel_id=1, replica_groups=mesh['grp'=16,'shard'=16] {'grp','shard'}, use_global_device_ids=true, to_apply=%region_10.11 | all-reduce | flops 256 | bytes 2048 | tf_op jit(solution)/shard_map/psum | solution.py:55
  191.1 161.8 %all-reduce.12.cloned.1.call-done = (f32[2,256,128]{2,0,1:T(2,128)}, f32[2,128,128]{2,1,0:T(8,128)}) async-done(((f32[2,256,128]{2,0,1:T(2,128)}, f32[2,128,128]{2,1,0:T(8,128)}), (f32[2,256,128]{2,0,1:T(2,128)}, f32[2,128,128]{2,1,0:T(8,128)})) %all-reduce.12.cloned.1.call-update) | async-done | bytes 393232 | tf_op jit(solution)/shard_map/psum | solution.py:55
  352.9 1.7 copy.117
  354.6 138.7 %all-reduce.10.cloned.1.call-done = bf16[16,256,128]{2,1,0:T(8,128)(2,1)} async-done(((bf16[16,256,128]{2,1,0:T(8,128)(2,1)}), bf16[16,256,128]{2,1,0:T(8,128)(2,1)}) %all-reduce.10.cloned.1.call-update) | async-done | bytes 1048592 | tf_op jit(solution)/shard_map/psum | solution.py:58
  493.3 2.8 convert_element_type.160
  496.1 0.7 copy.144
  (59 shorter events, 0.2 us)
Async XLA Ops:
  7.2 12.9 %copy-start = (bf16[2,256,128]{2,1,0:T(8,128)(2,1)S(1)}, bf16[2,256,128]{2,1,0:T(8,128)(2,1)}, u32[]{:S(2)}) copy-start(bf16[2,256,128]{2,1,0:T(8,128)(2,1)} %param.12) | copy-start | bytes 393220
  8.1 3.1 copy-start.16
  11.1 8.9 %copy-start.26 = (s32[256]{0:T(256)S(1)}, s32[256]{0:T(256)}, u32[]{:S(2)}) copy-start(s32[256]{0:T(256)} %param.11) | copy-start | bytes 3076
  11.1 10.2 %copy-start.27 = (f32[2,128]{1,0:T(2,128)S(1)}, f32[2,128]{1,0:T(2,128)}, u32[]{:S(2)}) copy-start(f32[2,128]{1,0:T(2,128)} %param.14) | copy-start | bytes 3076
  11.2 30.0 %all-to-all-start = ((bf16[384,16,128]{2,1,0:T(8,128)(2,1)}), bf16[384,16,128]{2,1,0:T(8,128)(2,1)S(1)}, u32[]{:S(2)}, u32[]{:S(2)}) async-start(bf16[384,16,128]{2,1,0:T(8,128)(2,1)} %multiply_convert_fusion.4), calls=%async_computation | async-start | bytes 3145728 | tf_op jit(solution)/shard_map/all_to_all | solution.py:34
  41.6 2.4 copy-start.1
  43.4 1.4 copy-start.14
  43.4 1.4 copy-start.23
  44.8 1.2 copy-start.8
  45.9 17.5 %copy-start.18 = (f32[24,256]{1,0:T(8,128)}, f32[24,256]{1,0:T(8,128)S(1)}, u32[]{:S(2)}) copy-start(f32[24,256]{1,0:T(8,128)S(1)} %fusion.43) | copy-start | bytes 73732
  46.7 7.4 %copy-start.3 = (bf16[24,256,128]{1,2,0:T(8,128)(2,1)}, bf16[24,256,128]{1,2,0:T(8,128)(2,1)S(1)}, u32[]{:S(2)}) copy-start(bf16[24,256,128]{1,2,0:T(8,128)(2,1)S(1)} %multiply_convert_fusion.2) | copy-start | bytes 4718596
  47.9 1.1 copy-start.10
  48.0 2.0 copy-start.5
  49.1 7.1 %copy-start.4 = (f32[24,256,128]{1,2,0:T(8,128)}, f32[24,256,128]{1,2,0:T(8,128)S(1)}, u32[]{:S(2)}) copy-start(f32[24,256,128]{1,2,0:T(8,128)S(1)} %get-tuple-element.39) | copy-start | bytes 9437188
  49.1 7.1 %copy-start.20 = (f32[24,256]{1,0:T(8,128)}, f32[24,256]{1,0:T(8,128)S(1)}, u32[]{:S(2)}) copy-start(f32[24,256]{1,0:T(8,128)S(1)} %fusion.44) | copy-start | bytes 73732
  52.9 3.3 copy-start.24
  54.7 0.9 copy-start.11
  59.1 4.3 copy-start.6
  59.2 4.3 copy-start.21
  59.2 2.0 copy-start.2
  62.0 0.9 copy-start.12
  68.9 31.6 %all-to-all-start.1 = ((bf16[24,256,128]{2,0,1:T(8,128)(2,1)}), bf16[24,256,128]{2,0,1:T(8,128)(2,1)}, u32[]{:S(2)}, u32[]{:S(2)}) async-start(bf16[24,256,128]{2,0,1:T(8,128)(2,1)} %copy.105), calls=%async_computation.1 | async-start | bytes 3145728 | tf_op jit(solution)/shard_map/all_to_all | solution.py:47
  73.3 279.5 %all-reduce.12.cloned.1.call-start = ((), (), s32[]{:S(2)}) async-start(), calls=%async_computation.3 | async-start | bytes 786432 | tf_op jit(solution)/shard_map/psum | solution.py:55
  94.5 4.2 copy-start.15
  94.5 4.2 copy-start.7
  94.5 4.2 copy-start.9
  94.5 4.2 copy-start.19
  94.5 4.2 copy-start.22
  100.5 392.8 %all-reduce.10.cloned.1.call-start = ((), (), s32[]{:S(2)}) async-start(), calls=%async_computation.2 | async-start | bytes 2097152 | tf_op jit(solution)/shard_map/psum | solution.py:58
  102.7 0.9 copy-start.17
  103.6 1.0 copy-start.29
  106.1 2.6 copy-start.13
  108.7 1.6 copy-start.28
  352.9 143.2 %copy-start.25 = (f32[2,128,128]{2,1,0:T(8,128)S(1)}, f32[2,128,128]{2,1,0:T(8,128)}, u32[]{:S(2)}) copy-start(f32[2,128,128]{2,1,0:T(8,128)} %get-tuple-element.44) | copy-start | bytes 393220
Sparse Core Ops, SparseCore 0:
  100.6 252.1 all-reduce.11
  355.5 137.7 all-reduce.9
where the time goes:
time: 506 us; the launch traced here: 504 us
  waiting for transfers between devices  320 us (63%)
  blocking collectives  80.8 us (16%)
  local copies, waits for them, and re-layouts  37.3 us (7%)
  matrix products  28.1 us (6%)
  between operations  14.6 us (3%)
  other arithmetic  11.7 us (2%)
  starting transfers between devices  10.8 us (2%)
    psum x1, waiting for transfers between devices, on_device(): lax.psum((compress_part, expand_part, grad_g), ('grp', 'shard'))  162 us
    psum x1, waiting for transfers between devices, on_device(): lax.psum(table_part.astype(jnp.bfloat16), 'grp').astype(jnp.float32)  139 us
    psum x1, blocking collectives, on_device(): lax.psum((compress_part, expand_part, grad_g), ('grp', 'shard'))  80.8 us
    all_to_all x1, waiting for transfers between devices, on_device(): lax.all_to_all(scaled, 'shard', split_axis=0, concat_axis=1, tiled=True)  19.7 us
    scatter x1, local copies, waits for them, and re-layouts, on_device(): compress_part = jnp.zeros((depth, features, width_k), jnp.float32).at[:,...  15.7 us
    unnamed x65, local copies, waits for them, and re-layouts  12.5 us
  transfers between devices with their start and end apart: 4, of which 3 were waited for; matrix products, arithmetic and copies ran while one was open for 8% of the time, Pallas kernels for 0%

commit v1 on v0

v1 whole, which is shorter than its diff:
```python
import jax
import jax.numpy as jnp
from jax import lax
from jax.sharding import Mesh, PartitionSpec as P

R = 256
SHARD = ("y", "xh", "core")
PLANE = ("xl", "y", "xh", "core")


def layers(x, wcol, expand_w, norm_gain):
    depth = wcol.shape[0]
    width = x.shape[2]
    for layer in range(depth):
        u_mat = jnp.einsum(
            "bfd,fk->bdk", x, wcol[layer], preferred_element_type=jnp.float32
        ).astype(jnp.bfloat16)
        inter = (
            jnp.einsum("bfd,bdk->bfk", x, u_mat, preferred_element_type=jnp.float32)
            / jnp.sqrt(jnp.float32(width))
        ).astype(jnp.bfloat16)
        mixed = x.astype(jnp.float32) + jnp.einsum(
            "bfk,kd->bfd", inter, expand_w[layer], preferred_element_type=jnp.float32
        )
        scale = lax.rsqrt(jnp.mean(mixed * mixed, axis=-1, keepdims=True) + 1e-06)
        x = (mixed * scale * norm_gain[layer]).astype(jnp.bfloat16)
    return x


def shift_z(x, step):
    return lax.ppermute(x, "z", [(i, (i + step) % 8) for i in range(8)])


def swap_xl(x):
    return lax.ppermute(x, "xl", [(0, 1), (1, 0)])


def on_device(pooled, row_scale, row_ids, feature_order, compress_w, expand_w, norm_gain, out_grad):
    bf16, f32 = jnp.bfloat16, jnp.float32
    xl = lax.axis_index("xl")
    z = lax.axis_index("z")
    place = (feature_order[None, :] == jnp.arange(256, dtype=jnp.int32)[:, None]).astype(bf16)
    wcol = jnp.einsum("fj,lfk->ljk", place, compress_w, preferred_element_type=f32).astype(bf16)
    scaled = (pooled.astype(f32) * row_scale[:, :, None]).astype(bf16)
    x_zero = lax.all_to_all(scaled, SHARD, split_axis=0, concat_axis=1, tiled=True)

    marks = jnp.stack([row_ids.astype(f32), row_scale]).transpose(0, 2, 1).reshape(2, 2, 8, 384)
    mine = lax.dynamic_index_in_dim(marks, xl, 1, keepdims=False)
    other = swap_xl(lax.dynamic_index_in_dim(marks, 1 - xl, 1, keepdims=False))
    low = xl == 0
    marks = jnp.concatenate([jnp.where(low, mine, other), jnp.where(low, other, mine)], axis=2)

    features_out, pull = jax.vjp(layers, x_zero, wcol, expand_w, norm_gain)
    grad_x, grad_w, grad_v, grad_g = pull(out_grad)
    compress_part = jnp.einsum("fj,ljk->lfk", place, grad_w, preferred_element_type=f32).astype(bf16)
    gain_high = grad_g.astype(bf16)
    gain_low = (grad_g - gain_high.astype(f32)).astype(bf16)
    dense = jnp.concatenate(
        [compress_part.reshape(512, 128), grad_v.reshape(256, 128), gain_high, gain_low, jnp.zeros((252, 128), bf16)]
    )
    parcels = grad_x.reshape(24, 16, 2, 8, 128).transpose(2, 1, 0, 3, 4).reshape(32, 192, 128)
    parcels = jnp.concatenate([parcels, dense.reshape(32, 32, 128)], axis=1)
    parcels = lax.all_to_all(parcels, PLANE, split_axis=0, concat_axis=0, tiled=True)

    dense_part = jnp.sum(parcels[:, 192:].astype(f32), axis=0).astype(bf16)
    grads = parcels[:, :192].reshape(768, 8, 128)
    hit = marks[0][:, None, :] == jnp.arange(R, dtype=f32)[None, :, None]
    scale_high = marks[1].astype(bf16)
    scale_low = (marks[1] - scale_high.astype(f32)).astype(bf16)
    none = jnp.zeros((), bf16)
    high = jnp.einsum("frb,bfd->frd", jnp.where(hit, scale_high[:, None, :], none), grads, preferred_element_type=f32)
    low_part = jnp.einsum("frb,bfd->frd", jnp.where(hit, scale_low[:, None, :], none), grads, preferred_element_type=f32)
    table_part = (high + low_part).astype(bf16)
    table_part = jnp.concatenate([table_part, jnp.broadcast_to(dense_part[None], (8, 32, 128))], axis=1)
    table_part = lax.all_to_all(table_part, "z", split_axis=0, concat_axis=0, tiled=True)
    summed = jnp.sum(table_part.astype(f32), axis=0).astype(bf16)
    table, dense_sum = summed[:256], summed[256:]

    dense_all = lax.all_to_all(
        jnp.broadcast_to(dense_sum[None], (32, 32, 128)), PLANE, split_axis=0, concat_axis=0, tiled=True
    ).reshape(1024, 128).astype(f32)
    compress_grad = dense_all[:512].reshape(2, 256, 128)
    expand_grad = dense_all[512:768].reshape(2, 128, 128)
    gain_grad = dense_all[768:770] + dense_all[770:772]

    other = swap_xl(table)
    pair = jnp.stack([jnp.where(low, table, other), jnp.where(low, other, table)])
    out = jnp.zeros((2, 8, R, 128), f32)

    def put(out, block, owner, start=0):
        return lax.dynamic_update_slice(out, block.astype(f32)[:, None], (0, owner % 8, start, 0))

    out = put(out, pair, z)
    up = down = pair
    for step in range(1, 4):
        up, down = shift_z(up, 1), shift_z(down, -1)
        out = put(out, up, z - step + 8)
        out = put(out, down, z + step)
    half_up = shift_z(up[:, :128], 1)
    half_down = shift_z(down[:, 128:], -1)
    out = put(out, half_up, z + 4)
    out = put(out, half_down, z + 4, 128)
    table_grad = out.reshape(16, R, 128)
    return (features_out, table_grad, compress_grad, expand_grad, gain_grad)


def solution(mesh):
    split = Mesh(mesh.devices.reshape(8, 2, 4, 2, 2), ("z", "xl", "y", "xh", "core"))
    grp = ("z", "xl")
    return jax.shard_map(
        on_device,
        mesh=split,
        in_specs=(
            P(grp, SHARD, None),
            P(grp, SHARD),
            P(grp, SHARD),
            P(),
            P(),
            P(),
            P(),
            P(grp + SHARD, None, None),
        ),
        out_specs=(P(grp + SHARD, None, None), P(SHARD, None, None), P(), P(), P()),
        check_vma=False,
    )
```

time: 506 us -> 171 us (0.34)
  waiting for transfers between devices: 320 us -> 64.3 us
  blocking collectives: 80.8 us -> 27.2 us
  local copies, waits for them, and re-layouts: 37.3 us -> 8.39 us
  starting transfers between devices: 10.8 us -> 28.3 us
  between operations: 14.6 us -> 1.25 us
    psum x2 -> x0, waiting for transfers between devices: 300 us -> none  [the longest x1 162 us: on_device(): lax.psum((compress_part, expand_part, grad_g), ('grp', 'shard'))]
    psum x1 -> x0, blocking collectives: 80.8 us -> none  [on_device(): lax.psum((compress_part, expand_part, grad_g), ('grp', 'shard'))]
    ppermute x0 -> x10, waiting for transfers between devices: none -> 32.5 us  [the longest x2 23.8 us: swap_xl(): return lax.ppermute(x, 'xl', [(0, 1), (1, 0)])]
    all_to_all x0 -> x1, blocking collectives: none -> 27.2 us  [on_device(): lax.all_to_all(table_part, 'z', split_axis=0, concat_axis=0, tiled=True)]
    scatter x1 -> x0, local copies, waits for them, and re-layouts: 15.7 us -> none  [on_device(): compress_part = jnp.zeros((depth, features, width_k), jnp.float32).at[:,...]
    all_to_all x2 -> x3, waiting for transfers between devices: 19.7 us -> 31.8 us  [the longest x1 23.4 us: on_device(): lax.all_to_all(scaled, SHARD, split_axis=0, concat_axis=1, tiled=True)]
    ppermute x0 -> x10, starting transfers between devices: none -> 11.1 us  [the longest x8 9.04 us: shift_z(): return lax.ppermute(x, 'z', [(i, (i + step) % 8) for i in range(8)])]
    unnamed x65 -> x23, local copies, waits for them, and re-layouts: 12.5 us -> 3.48 us
  transfers between devices with their start and end apart: 4 -> 13, of which waited for: 3 -> 7; matrix products, arithmetic and copies ran while one was open for 8% -> 2% of each run, Pallas kernels for 0% -> 0%
where the time goes in v1:
time: 171 us; the launch traced here: 170 us
  waiting for transfers between devices  64.3 us (38%)
  matrix products  31.3 us (18%)
  starting transfers between devices  28.3 us (17%)
  blocking collectives  27.2 us (16%)
  other arithmetic  9.37 us (5%)
  local copies, waits for them, and re-layouts  8.39 us (5%)
    all_to_all x1, blocking collectives, on_device(): lax.all_to_all(table_part, 'z', split_axis=0, concat_axis=0, tiled=True)  27.2 us
    ppermute x2, waiting for transfers between devices, swap_xl(): return lax.ppermute(x, 'xl', [(0, 1), (1, 0)])  23.8 us
    all_to_all x1, waiting for transfers between devices, on_device(): lax.all_to_all(scaled, SHARD, split_axis=0, concat_axis=1, tiled=True)  23.4 us
    dot_general x6, matrix products, layers(): jnp.einsum('bfk,kd->bfd', inter, expand_w[layer], preferred_element_type=...  12.3 us
    dot_general x6, matrix products, layers(): jnp.einsum('bfd,bdk->bfk', x, u_mat, preferred_element_type=jnp.float32)  11.2 us
    ppermute x8, starting transfers between devices, shift_z(): return lax.ppermute(x, 'z', [(i, (i + step) % 8) for i in range(8)])  9.04 us
    ppermute x8, waiting for transfers between devices, shift_z(): return lax.ppermute(x, 'z', [(i, (i + step) % 8) for i in range(8)])  8.71 us
    all_to_all x1, starting transfers between devices, on_device(): lax.all_to_all(scaled, SHARD, split_axis=0, concat_axis=1, tiled=True)  6.14 us
  transfers between devices with their start and end apart: 13, of which 7 were waited for; matrix products, arithmetic and copies ran while one was open for 2% of the time, Pallas kernels for 0%

profile of v1, /device:TPU:2, one launch (start us, length us, event | category | flops | bytes accessed | tf_op | source)
XLA Modules:
  0.0 170.1 jit_solution(16110444517697002270)
XLA Ops:
  0.6 0.0 copy-start
  0.6 0.9 copy.62
  1.6 3.0 %multiply_convert_fusion.4 = bf16[384,16,128]{2,1,0:T(8,128)(2,1)} fusion(bf16[384,16,128]{2,1,0:T(8,128)(2,1)} %param.8, f32[384,16]{1,0:T(8,128)S(1)} %copy.62), kind=kLoop, calls=%fused_computation.35 | loop fusion | flops 2359296 | bytes 3170304 | tf_op jit(solution)/shard_map/convert_element_type | solution.py:44
  4.6 6.1 %all-to-all-start = ((bf16[384,16,128]{2,1,0:T(8,128)(2,1)}), bf16[384,16,128]{2,1,0:T(8,128)(2,1)S(1)}, u32[]{:S(2)}, u32[]{:S(2)}) async-start(bf16[384,16,128]{2,1,0:T(8,128)(2,1)} %multiply_convert_fusion.4), calls=%async_computation | async-start | bytes 3145728 | tf_op jit(solution)/shard_map/all_to_all | solution.py:45
  10.7 0.3 fusion.44
  11.0 23.4 %all-to-all-done = bf16[384,16,128]{2,1,0:T(8,128)(2,1)S(1)} async-done(((bf16[384,16,128]{2,1,0:T(8,128)(2,1)}), bf16[384,16,128]{2,1,0:T(8,128)(2,1)S(1)}, u32[]{:S(2)}, u32[]{:S(2)}) %all-to-all-start) | async-done | bytes 1572896 | tf_op jit(solution)/shard_map/all_to_all | solution.py:45
  34.4 0.4 copy.63
  34.9 0.6 convolution_convert_fusion.5
  35.5 0.9 copy-done.2
  36.4 0.6 multiply_convert_fusion.3
  37.0 1.1 multiply_reduce_fusion.1
  38.1 1.0 multiply_convert_fusion.2
  39.1 0.6 convolution_convert_fusion.4
  39.8 0.6 multiply_convert_fusion.1
  40.3 1.0 multiply_reduce_fusion
  41.4 0.3 copy-done.4
  41.7 2.9 %fusion.8 = (f32[128]{0:T(128)S(1)}, f32[24,256]{1,0:T(8,128)S(1)}, bf16[24,256,128]{2,1,0:T(8,128)(2,1)}) fusion(bf16[24,256,128]{2,1,0:T(8,128)(2,1)S(1)} %copy-done.4, f32[24,256,128]{2,1,0:T(8,128)S(1)} %get-tuple-element.28, f32[24,256]{1,0:T(8,128)S(1)} %fusion.78, f32[128]{0:T(128)S(1)} %get-tuple-element.23), kind=kLoop, calls=%fused_computation.15 | loop fusion | flops 7071616 | bytes 6341632 | tf_op jit(solution)/shard_map/transpose(jvp())/reduce_sum | solution.py:26
  44.7 2.7 %fusion.53 = bf16[1,128,128]{2,1,0:T(8,128)(2,1)S(1)} fusion(bf16[24,256,128]{2,1,0:T(8,128)(2,1)S(1)} %multiply_convert_fusion.1, bf16[24,256,128]{2,1,0:T(8,128)(2,1)S(1)} %copy-done.4, f32[24,256,128]{2,1,0:T(8,128)S(1)} %get-tuple-element.28, f32[24,256]{1,0:T(8,128)S(1)} %multiply_multiply_fusion.1, f32[128]{0:T(128)S(1)} %get-tuple-element.23, ...), kind=kOutput, calls=%fused_computation.76 | convolution fusion | flops 206061568 | bytes 6373888 | tf_op jit(solution)/shard_map/transpose(jvp(bfk,kd->bfd))/dot_general | solution.py:22
  47.3 2.5 %convolution_convert_fusion.3 = bf16[24,256,128]{2,1,0:T(8,128)(2,1)S(1)} fusion(bf16[2,128,128]{2,1,0:T(8,128)(2,1)S(1)} %copy-done.6, bf16[24,256,128]{2,1,0:T(8,128)(2,1)S(1)} %copy-done.4, f32[24,256,128]{2,1,0:T(8,128)S(1)} %get-tuple-element.28, f32[24,256]{1,0:T(8,128)S(1)} %multiply_multiply_fusion.1, f32[128]{0:T(128)S(1)} %get-tuple-element.23, ...), kind=kOutput, calls=%fused_computation.42 | convolution fusion | flops 206831616 | bytes 6373888 | tf_op jit(solution)/shard_map/transpose(jvp(bfk,kd->bfd))/dot_general | solution.py:22
  49.8 0.8 fusion.30
  50.6 0.6 fusion.49
  51.2 0.6 convolution_convert_fusion.2
  51.8 4.6 %fusion.9 = (f32[128]{0:T(128)S(1)}, f32[24,256]{1,0:T(8,128)S(1)}, bf16[24,256,128]{2,1,0:T(8,128)(2,1)S(1)}) fusion(f32[24,256,128]{2,1,0:T(8,128)S(1)} %get-tuple-element.26, f32[24,256]{1,0:T(8,128)S(1)} %fusion.77, f32[128]{0:T(128)S(1)} %get-tuple-element.24, bf16[24,128,256]{1,2,0:T(8,128)(2,1)S(1)} %convolution_convert_fusion.2, ...), kind=kOutput, calls=%fused_computation.16 | convolution fusion | flops 216262528 | bytes 13469184 | tf_op jit(solution)/shard_map/transpose(jvp(bfd,bdk->bfk))/dot_general | solution.py:19
  56.4 2.5 %fusion.52 = bf16[1,128,128]{2,1,0:T(8,128)(2,1)S(1)} fusion(bf16[24,256,128]{2,1,0:T(8,128)(2,1)S(1)} %multiply_convert_fusion.3, bf16[24,256,128]{2,1,0:T(8,128)(2,1)S(1)} %get-tuple-element.29, f32[24,256,128]{2,1,0:T(8,128)S(1)} %get-tuple-element.26, f32[24,256]{1,0:T(8,128)S(1)} %multiply_multiply_fusion, f32[128]{0:T(128)S(1)} %get-tuple-element.24, ...), kind=kOutput, calls=%fused_computation.75 | convolution fusion | flops 206061568 | bytes 6373888 | tf_op jit(solution)/shard_map/transpose(jvp(bfk,kd->bfd))/dot_general | solution.py:22
  59.0 2.5 %convolution_convert_fusion.1 = bf16[24,256,128]{2,1,0:T(8,128)(2,1)S(1)} fusion(bf16[2,128,128]{2,1,0:T(8,128)(2,1)S(1)} %copy-done.6, bf16[24,256,128]{2,1,0:T(8,128)(2,1)S(1)} %get-tuple-element.29, f32[24,256,128]{2,1,0:T(8,128)S(1)} %get-tuple-element.26, f32[24,256]{1,0:T(8,128)S(1)} %multiply_multiply_fusion, f32[128]{0:T(128)S(1)} %get-tuple-element.24, ...), kind=kOutput, calls=%fused_computation.40 | convolution fusion | flops 206831616 | bytes 6373888 | tf_op jit(solution)/shard_map/transpose(jvp(bfk,kd->bfd))/dot_general | solution.py:22
  61.5 0.8 fusion.31
  62.3 0.6 fusion.48
  62.9 1.7 %convolution_convert_fusion = bf16[24,128,256]{1,2,0:T(8,128)(2,1)} fusion(bf16[24,128,128]{2,1,0:T(8,128)(2,1)S(1)} %fusion.31, bf16[2,256,128]{2,1,0:T(8,128)(2,1)S(1)} %fusion.44), kind=kOutput, calls=%fused_computation.39 | convolution fusion | flops 202113024 | bytes 2424832 | tf_op jit(solution)/shard_map/transpose(jvp(bfd,fk->bdk))/dot_general | solution.py:15
  64.6 0.9 fusion.45
  65.5 1.0 copy.73
  66.5 3.8 %bitcast_add_fusion = bf16[24,256,128]{2,1,0:T(8,128)(2,1)S(1)} fusion(bf16[24,128,256]{1,2,0:T(8,128)(2,1)} %convolution_convert_fusion, bf16[24,128,128]{2,1,0:T(8,128)(2,1)} %copy-done.2, bf16[24,256,128]{2,1,0:T(8,128)(2,1)} %copy-done.1, f32[24,256,128]{2,1,0:T(8,128)S(1)} %get-tuple-element.26, f32[24,256]{1,0:T(8,128)S(1)} %multiply_multiply_fusion, ...), kind=kOutput, calls=%fused_computation.43 | convolution fusion | flops 210763776 | bytes 10273280 | tf_op jit(solution)/shard_map/transpose(jvp(bfd,bdk->bfk))/dot_general | solution.py:19
  70.3 0.4 copy.71
  70.8 0.5 concatenate.20
  71.3 1.3 pad_maximum_fusion
  72.7 5.1 %all-to-all-start.1 = ((bf16[32,224,128]{2,1,0:T(8,128)(2,1)}), bf16[32,224,128]{2,1,0:T(8,128)(2,1)S(1)}, u32[]{:S(2)}, u32[]{:S(2)}) async-start(bf16[32,224,128]{2,1,0:T(8,128)(2,1)} %pad_maximum_fusion), calls=%async_computation.1 | async-start | bytes 3670016 | tf_op jit(solution)/shard_map/all_to_all | solution.py:63
  77.9 0.3 collective-permute-start
  78.2 21.2 %collective-permute-done = f32[2,8,384]{2,1,0:T(8,128)S(1)} collective-permute-done((f32[2,8,384]{2,1,0:T(8,128)S(1)}, f32[2,8,384]{2,1,0:T(8,128)S(1)}, u32[]{:S(2)}, u32[]{:S(2)}) %collective-permute-start) | collective-permute-done | bytes 24608 | tf_op jit(solution)/shard_map/ppermute | solution.py:35
  99.4 2.9 %all-to-all-done.1 = bf16[32,224,128]{2,1,0:T(8,128)(2,1)S(1)} async-done(((bf16[32,224,128]{2,1,0:T(8,128)(2,1)}), bf16[32,224,128]{2,1,0:T(8,128)(2,1)S(1)}, u32[]{:S(2)}, u32[]{:S(2)}) %all-to-all-start.1) | async-done | bytes 1835040 | tf_op jit(solution)/shard_map/all_to_all | solution.py:63
  102.4 0.2 slice.79
  102.5 1.0 fusion.10
  103.6 1.0 fusion.39
  104.6 0.1 slice_reduce_fusion
  104.7 27.2 %all_to_all.33 = bf16[8,288,128]{2,1,0:T(8,128)(2,1)S(1)} all-to-all(bf16[8,288,128]{2,1,0:T(8,128)(2,1)S(1)} %pad_maximum_fusion.1), channel_id=1, replica_groups=mesh['z'=8,'xl'=2,'y'=4,'xh'=2,'core'=2] {'z'}, dimensions={0} | all-to-all | bytes 1179648 | tf_op jit(solution)/shard_map/all_to_all | solution.py:75
  131.9 0.1 reduce_sum.101
  132.0 1.7 %collective-permute-start.1 = (bf16[256,128]{1,0:T(8,128)(2,1)S(1)}, bf16[256,128]{1,0:T(8,128)(2,1)S(1)}, u32[]{:S(2)}, u32[]{:S(2)}) collective-permute-start(bf16[256,128]{1,0:T(8,128)(2,1)S(1)} %slice.81), channel_id=1, source_target_pairs={{0,16},{16,0},{1,17},{17,1},{2,18},{18,2},{3,19},{19,3},{4,20},{20... | collective-permute-start | bytes 196616 | tf_op jit(solution)/shard_map/ppermute | solution.py:35
  133.7 2.6 %collective-permute-done.1 = bf16[256,128]{1,0:T(8,128)(2,1)S(1)} collective-permute-done((bf16[256,128]{1,0:T(8,128)(2,1)S(1)}, bf16[256,128]{1,0:T(8,128)(2,1)S(1)}, u32[]{:S(2)}, u32[]{:S(2)}) %collective-permute-start.1) | collective-permute-done | bytes 65568 | tf_op jit(solution)/shard_map/ppermute | solution.py:35
  136.4 0.1 collective-permute-start.3
  136.5 2.0 %collective-permute-start.2 = (bf16[2,256,128]{2,1,0:T(8,128)(2,1)S(1)}, bf16[2,256,128]{2,1,0:T(8,128)(2,1)S(1)}, u32[]{:S(2)}, u32[]{:S(2)}) collective-permute-start(bf16[2,256,128]{2,1,0:T(8,128)(2,1)S(1)} %pad_maximum_fusion.2), channel_id=1, source_target_pairs={{0,32},{32,64},{64,96},{96,128},{128,160},{160,192},{192,224},{224... | collective-permute-start | bytes 393224 | tf_op jit(solution)/shard_map/ppermute | solution.py:31
  138.5 0.7 broadcast_in_dim.147
  139.3 5.9 %all-to-all-start.3 = ((bf16[32,32,128]{2,1,0:T(8,128)(2,1)}), bf16[32,32,128]{2,1,0:T(8,128)(2,1)S(1)}, u32[]{:S(2)}, u32[]{:S(2)}) async-start(bf16[32,32,128]{2,1,0:T(8,128)(2,1)} %broadcast_in_dim.147), calls=%async_computation.3 | async-start | bytes 524288 | tf_op jit(solution)/shard_map/all_to_all | solution.py:79
  145.2 0.2 broadcast_in_dim.117
  145.4 1.6 collective-permute-start.5
  147.0 0.5 collective-permute-start.4
  147.6 5.4 %all-to-all-done.3 = bf16[32,32,128]{2,1,0:T(8,128)(2,1)S(1)} async-done(((bf16[32,32,128]{2,1,0:T(8,128)(2,1)}), bf16[32,32,128]{2,1,0:T(8,128)(2,1)S(1)}, u32[]{:S(2)}, u32[]{:S(2)}) %all-to-all-start.3) | async-done | bytes 262176 | tf_op jit(solution)/shard_map/all_to_all | solution.py:79
  153.0 0.7 slice.86
  153.7 0.7 slice.85
  154.4 0.6 slice_add_fusion
  155.0 1.5 collective-permute-start.7
  156.5 0.5 collective-permute-start.6
  157.1 3.3 %collective-permute-done.7 = bf16[2,256,128]{2,1,0:T(8,128)(2,1)S(1)} collective-permute-done((bf16[2,256,128]{2,1,0:T(8,128)(2,1)S(1)}, bf16[2,256,128]{2,1,0:T(8,128)(2,1)S(1)}, u32[]{:S(2)}, u32[]{:S(2)}) %collective-permute-start.7) | collective-permute-done | bytes 131104 | tf_op jit(solution)/shard_map/ppermute | solution.py:31
  160.4 2.7 %collective-permute-start.9 = (bf16[2,128,128]{2,1,0:T(8,128)(2,1)S(1)}, bf16[2,128,128]{2,1,0:T(8,128)(2,1)S(1)}, u32[]{:S(2)}, u32[]{:S(2)}) collective-permute-start(bf16[2,128,128]{2,1,0:T(8,128)(2,1)S(1)} %slice.83), channel_id=1, source_target_pairs={{0,224},{32,0},{64,32},{96,64},{128,96},{160,128},{192,160},{224,1... | collective-permute-start | bytes 196616 | tf_op jit(solution)/shard_map/ppermute | solution.py:31
  163.1 0.1 collective-permute-start.8
  163.3 5.4 %collective-permute-done.8 = bf16[2,128,128]{2,1,0:T(8,128)(2,1)S(1)} collective-permute-done((bf16[2,128,128]{2,1,0:T(8,128)(2,1)S(1)}, bf16[2,128,128]{2,1,0:T(8,128)(2,1)S(1)}, u32[]{:S(2)}, u32[]{:S(2)}) %collective-permute-start.8) | collective-permute-done | bytes 65568 | tf_op jit(solution)/shard_map/ppermute | solution.py:31
  168.8 1.3 copy-done.5
  (57 shorter events, 0.6 us)
Async XLA Ops:
  0.6 10.1 %copy-start = (bf16[2,256,128]{2,1,0:T(8,128)(2,1)S(1)}, bf16[2,256,128]{2,1,0:T(8,128)(2,1)}, u32[]{:S(2)}) copy-start(bf16[2,256,128]{2,1,0:T(8,128)(2,1)} %param.12) | copy-start | bytes 393220
  1.5 9.2 %copy-start.10 = (f32[2,128]{1,0:T(2,128)S(1)}, f32[2,128]{1,0:T(2,128)}, u32[]{:S(2)}) copy-start(f32[2,128]{1,0:T(2,128)} %param.14) | copy-start | bytes 3076
  1.6 9.2 %copy-start.9 = (s32[256]{0:T(256)S(1)}, s32[256]{0:T(256)}, u32[]{:S(2)}) copy-start(s32[256]{0:T(256)} %param.11) | copy-start | bytes 3076
  4.6 29.9 %all-to-all-start = ((bf16[384,16,128]{2,1,0:T(8,128)(2,1)}), bf16[384,16,128]{2,1,0:T(8,128)(2,1)S(1)}, u32[]{:S(2)}, u32[]{:S(2)}) async-start(bf16[384,16,128]{2,1,0:T(8,128)(2,1)} %multiply_convert_fusion.4), calls=%async_computation | async-start | bytes 3145728 | tf_op jit(solution)/shard_map/all_to_all | solution.py:45
  34.9 2.1 %copy-start.6 = (bf16[2,128,128]{2,1,0:T(8,128)(2,1)S(1)}, bf16[2,128,128]{2,1,0:T(8,128)(2,1)}, u32[]{:S(2)}) copy-start(bf16[2,128,128]{2,1,0:T(8,128)(2,1)} %param.13) | copy-start | bytes 196612
  35.5 0.9 copy-start.2
  40.3 1.4 copy-start.4
  56.4 2.6 %copy-start.3 = (bf16[24,256,128]{2,1,0:T(8,128)(2,1)}, bf16[24,256,128]{2,1,0:T(8,128)(2,1)S(1)}, u32[]{:S(2)}) copy-start(bf16[24,256,128]{2,1,0:T(8,128)(2,1)S(1)} %get-tuple-element.29) | copy-start | bytes 4718596
  61.5 1.4 copy-start.1
  71.3 6.5 %copy-start.8 = (s32[384,16]{0,1:T(8,128)S(1)}, s32[384,16]{0,1:T(8,128)}, u32[]{:S(2)}) copy-start(s32[384,16]{0,1:T(8,128)} %param.10) | copy-start | bytes 73732
  71.3 6.5 %copy-start.7 = (f32[384,16]{0,1:T(8,128)S(1)}, f32[384,16]{0,1:T(8,128)}, u32[]{:S(2)}) copy-start(f32[384,16]{0,1:T(8,128)} %param.9) | copy-start | bytes 73732
  72.7 29.7 %all-to-all-start.1 = ((bf16[32,224,128]{2,1,0:T(8,128)(2,1)}), bf16[32,224,128]{2,1,0:T(8,128)(2,1)S(1)}, u32[]{:S(2)}, u32[]{:S(2)}) async-start(bf16[32,224,128]{2,1,0:T(8,128)(2,1)} %pad_maximum_fusion), calls=%async_computation.1 | async-start | bytes 3670016 | tf_op jit(solution)/shard_map/all_to_all | solution.py:63
  77.9 21.5 %collective-permute-start = (f32[2,8,384]{2,1,0:T(8,128)S(1)}, f32[2,8,384]{2,1,0:T(8,128)S(1)}, u32[]{:S(2)}, u32[]{:S(2)}) collective-permute-start(f32[2,8,384]{2,1,0:T(8,128)S(1)} %dynamic-slice_bitcast_fusion), channel_id=1, source_target_pairs={{0,16},{16,0},{1,17},{17,1},{2,18},{18,2},{3,19},{19,3},{4,20},{20... | collective-permute-start | bytes 73736 | tf_op jit(solution)/shard_map/ppermute | solution.py:35
  132.0 4.4 %collective-permute-start.1 = (bf16[256,128]{1,0:T(8,128)(2,1)S(1)}, bf16[256,128]{1,0:T(8,128)(2,1)S(1)}, u32[]{:S(2)}, u32[]{:S(2)}) collective-permute-start(bf16[256,128]{1,0:T(8,128)(2,1)S(1)} %slice.81), channel_id=1, source_target_pairs={{0,16},{16,0},{1,17},{17,1},{2,18},{18,2},{3,19},{19,3},{4,20},{20... | collective-permute-start | bytes 196616 | tf_op jit(solution)/shard_map/ppermute | solution.py:35
  136.4 9.0 %collective-permute-start.3 = (bf16[2,256,128]{2,1,0:T(8,128)(2,1)S(1)}, bf16[2,256,128]{2,1,0:T(8,128)(2,1)S(1)}, u32[]{:S(2)}, u32[]{:S(2)}) collective-permute-start(bf16[2,256,128]{2,1,0:T(8,128)(2,1)S(1)} %pad_maximum_fusion.2), channel_id=1, source_target_pairs={{0,224},{32,0},{64,32},{96,64},{128,96},{160,128},{192,160},{224,1... | collective-permute-start | bytes 393224 | tf_op jit(solution)/shard_map/ppermute | solution.py:31
  136.5 10.5 %collective-permute-start.2 = (bf16[2,256,128]{2,1,0:T(8,128)(2,1)S(1)}, bf16[2,256,128]{2,1,0:T(8,128)(2,1)S(1)}, u32[]{:S(2)}, u32[]{:S(2)}) collective-permute-start(bf16[2,256,128]{2,1,0:T(8,128)(2,1)S(1)} %pad_maximum_fusion.2), channel_id=1, source_target_pairs={{0,32},{32,64},{64,96},{96,128},{128,160},{160,192},{192,224},{224... | collective-permute-start | bytes 393224 | tf_op jit(solution)/shard_map/ppermute | solution.py:31
  139.3 13.7 %all-to-all-start.3 = ((bf16[32,32,128]{2,1,0:T(8,128)(2,1)}), bf16[32,32,128]{2,1,0:T(8,128)(2,1)S(1)}, u32[]{:S(2)}, u32[]{:S(2)}) async-start(bf16[32,32,128]{2,1,0:T(8,128)(2,1)} %broadcast_in_dim.147), calls=%async_computation.3 | async-start | bytes 524288 | tf_op jit(solution)/shard_map/all_to_all | solution.py:79
  145.4 9.6 %collective-permute-start.5 = (bf16[2,256,128]{2,1,0:T(8,128)(2,1)S(1)}, bf16[2,256,128]{2,1,0:T(8,128)(2,1)S(1)}, u32[]{:S(2)}, u32[]{:S(2)}) collective-permute-start(bf16[2,256,128]{2,1,0:T(8,128)(2,1)S(1)} %collective-permute-done.3), channel_id=1, source_target_pairs={{0,224},{32,0},{64,32},{96,64},{128,96},{160,128},{192,160},{224,1... | collective-permute-start | bytes 393224 | tf_op jit(solution)/shard_map/ppermute | solution.py:31
  147.0 9.5 %collective-permute-start.4 = (bf16[2,256,128]{2,1,0:T(8,128)(2,1)S(1)}, bf16[2,256,128]{2,1,0:T(8,128)(2,1)S(1)}, u32[]{:S(2)}, u32[]{:S(2)}) collective-permute-start(bf16[2,256,128]{2,1,0:T(8,128)(2,1)S(1)} %collective-permute-done.2), channel_id=1, source_target_pairs={{0,32},{32,64},{64,96},{96,128},{128,160},{160,192},{192,224},{224... | collective-permute-start | bytes 393224 | tf_op jit(solution)/shard_map/ppermute | solution.py:31
  155.0 5.4 %collective-permute-start.7 = (bf16[2,256,128]{2,1,0:T(8,128)(2,1)S(1)}, bf16[2,256,128]{2,1,0:T(8,128)(2,1)S(1)}, u32[]{:S(2)}, u32[]{:S(2)}) collective-permute-start(bf16[2,256,128]{2,1,0:T(8,128)(2,1)S(1)} %collective-permute-done.5), channel_id=1, source_target_pairs={{0,224},{32,0},{64,32},{96,64},{128,96},{160,128},{192,160},{224,1... | collective-permute-start | bytes 393224 | tf_op jit(solution)/shard_map/ppermute | solution.py:31
  156.5 6.6 %collective-permute-start.6 = (bf16[2,256,128]{2,1,0:T(8,128)(2,1)S(1)}, bf16[2,256,128]{2,1,0:T(8,128)(2,1)S(1)}, u32[]{:S(2)}, u32[]{:S(2)}) collective-permute-start(bf16[2,256,128]{2,1,0:T(8,128)(2,1)S(1)} %collective-permute-done.4), channel_id=1, source_target_pairs={{0,32},{32,64},{64,96},{96,128},{128,160},{160,192},{192,224},{224... | collective-permute-start | bytes 393224 | tf_op jit(solution)/shard_map/ppermute | solution.py:31
  160.4 8.3 %collective-permute-start.9 = (bf16[2,128,128]{2,1,0:T(8,128)(2,1)S(1)}, bf16[2,128,128]{2,1,0:T(8,128)(2,1)S(1)}, u32[]{:S(2)}, u32[]{:S(2)}) collective-permute-start(bf16[2,128,128]{2,1,0:T(8,128)(2,1)S(1)} %slice.83), channel_id=1, source_target_pairs={{0,224},{32,0},{64,32},{96,64},{128,96},{160,128},{192,160},{224,1... | collective-permute-start | bytes 196616 | tf_op jit(solution)/shard_map/ppermute | solution.py:31
  163.1 5.6 %collective-permute-start.8 = (bf16[2,128,128]{2,1,0:T(8,128)(2,1)S(1)}, bf16[2,128,128]{2,1,0:T(8,128)(2,1)S(1)}, u32[]{:S(2)}, u32[]{:S(2)}) collective-permute-start(bf16[2,128,128]{2,1,0:T(8,128)(2,1)S(1)} %slice.82), channel_id=1, source_target_pairs={{0,32},{32,64},{64,96},{96,128},{128,160},{160,192},{192,224},{224... | collective-permute-start | bytes 196616 | tf_op jit(solution)/shard_map/ppermute | solution.py:31
  168.7 1.3 copy-start.5

commit v2 on v1

--- a/solution.py
+++ b/solution.py
@@ -1,6 +1,10 @@
+import math
+
 import jax
 import jax.numpy as jnp
 from jax import lax
+from jax.experimental import pallas as pl
+from jax.experimental.pallas import tpu as pltpu
 from jax.sharding import Mesh, PartitionSpec as P
 
 R = 256
@@ -8,23 +12,122 @@
 PLANE = ("xl", "y", "xh", "core")
 
 
-def layers(x, wcol, expand_w, norm_gain):
-    depth = wcol.shape[0]
-    width = x.shape[2]
-    for layer in range(depth):
-        u_mat = jnp.einsum(
-            "bfd,fk->bdk", x, wcol[layer], preferred_element_type=jnp.float32
-        ).astype(jnp.bfloat16)
-        inter = (
-            jnp.einsum("bfd,bdk->bfk", x, u_mat, preferred_element_type=jnp.float32)
-            / jnp.sqrt(jnp.float32(width))
-        ).astype(jnp.bfloat16)
-        mixed = x.astype(jnp.float32) + jnp.einsum(
-            "bfk,kd->bfd", inter, expand_w[layer], preferred_element_type=jnp.float32
-        )
-        scale = lax.rsqrt(jnp.mean(mixed * mixed, axis=-1, keepdims=True) + 1e-06)
-        x = (mixed * scale * norm_gain[layer]).astype(jnp.bfloat16)
-    return x
+def dot(a, b, dims=((1,), (0,))):
+    return lax.dot_general(a, b, (dims, ((), ())), preferred_element_type=jnp.float32)
+
+
+NT = ((1,), (1,))
+TN = ((0,), (0,))
+B = 4
+
+
+def layers_kernel(x_ref, og_ref, w_ref, wt_ref, v_ref, gain_ref, place_ref, feat_ref, out_ref, dw, dv, dg):
+    step = pl.program_id(0)
+    bf16, f32 = jnp.bfloat16, jnp.float32
+    root = 1.0 / math.sqrt(128.0)
+
+    @pl.when(step == 0)
+    def _():
+        dw[...] = jnp.zeros_like(dw)
+        dv[...] = jnp.zeros_like(dv)
+        dg[...] = jnp.zeros_like(dg)
+
+    x = [x_ref[:, b].reshape(256, 128) for b in range(B)]
+    saved = []
+    for layer in range(2):
+        gain = gain_ref[layer : layer + 1, :]
+        ut = [dot(wt_ref[layer], x[b]).astype(bf16) for b in range(B)]
+        inter = [(dot(x[b], ut[b], NT) * root).astype(bf16) for b in range(B)]
+        kept = []
+        after = []
+        for b in range(B):
+            z = x[b].astype(f32) + dot(inter[b], v_ref[layer])
+            r = lax.rsqrt(jnp.mean(z * z, axis=-1, keepdims=True) + 1e-06)
+            n = z * r
+            kept.append((n, r))
+            after.append((n * gain).astype(bf16))
+        saved.append((x, ut, inter, kept))
+        x = after
+    for b in range(B):
+        feat_ref[b] = x[b]
+    c = [og_ref[b].astype(f32) for b in range(B)]
+    for layer in (1, 0):
+        gain = gain_ref[layer : layer + 1, :]
+        x, ut, inter, kept = saved[layer]
+        below = []
+        dw_sum = 0.0
+        dv_sum = 0.0
+        dg_sum = 0.0
+        for b in range(B):
+            n, r = kept[b]
+            cn = c[b] * n
+            dg_sum = dg_sum + jnp.sum(cn.reshape(32, 8, 128), axis=0)
+            mean = jnp.mean(cn * gain, axis=-1, keepdims=True)
+            dz = r * (c[b] * gain - n * mean)
+            dzb = dz.astype(bf16)
+            dv_sum = dv_sum + dot(inter[b], dzb, TN)
+            dint = dot(dzb, v_ref[layer], NT).astype(bf16)
+            dut = dot(dint, x[b], TN).astype(bf16)
+            left = jnp.concatenate([dint, w_ref[layer]], axis=1)
+            right = jnp.concatenate([ut[b], dut], axis=0)
+            dx = (dz + dot(left, right) * root).astype(bf16)
+            dw_sum = dw_sum + dot(x[b], dut, NT)
+            below.append(dx.astype(f32))
+        dw[layer] += dw_sum
+        dv[layer] += dv_sum
+        dg[layer] += dg_sum
+        c = below
+    for b in range(0, B, 2):
+        first = c[b].reshape(16, 2, 8, 128)
+        second = c[b + 1].reshape(16, 2, 8, 128)
+        rows = pl.ds(pl.multiple_of(step * (B * 8) + b * 8, 16), 16)
+        for half in range(2):
+            both = jnp.concatenate([first[:, half], second[:, half]], axis=1)
+            out_ref[half * 16 : half * 16 + 16, rows, :] = both.astype(bf16)
+
+    @pl.when(step == pl.num_programs(0) - 1)
+    def _():
+        for layer in range(2):
+            grad = (dw[layer] * root).astype(bf16)
+            moved = dot(place_ref[...], grad).astype(bf16)
+            out_ref[layer * 8 : layer * 8 + 8, 192:224, :] = moved.reshape(8, 32, 128)
+            out_ref[16 + layer * 4 : 20 + layer * 4, 192:224, :] = dv[layer].astype(bf16).reshape(4, 32, 128)
+        total = jnp.sum(dg[...], axis=1)
+        high = total.astype(bf16).astype(f32)
+        rest = jnp.concatenate([high, total - high, jnp.zeros((28, 128), f32)], axis=0)
+        out_ref[24, 192:224, :] = rest.astype(bf16)
+        out_ref[25:32, 192:224, :] = jnp.zeros((7, 32, 128), bf16)
+
+
+def run_layers(x, out_grad, wcol, wcol_t, expand_w, norm_gain, place):
+    bf16, f32 = jnp.bfloat16, jnp.float32
+    whole = lambda *shape: pl.BlockSpec(shape, lambda i: (0,) * len(shape))
+    return pl.pallas_call(
+        layers_kernel,
+        grid=(24 // B,),
+        out_shape=(
+            jax.ShapeDtypeStruct((24, 256, 128), bf16),
+            jax.ShapeDtypeStruct((32, 224, 128), bf16),
+        ),
+        in_specs=[
+            pl.BlockSpec((16, B, 16, 128), lambda i: (0, i, 0, 0)),
+            pl.BlockSpec((B, 256, 128), lambda i: (i, 0, 0)),
+            whole(2, 256, 128),
+            whole(2, 128, 256),
+            whole(2, 128, 128),
+            whole(2, 128),
+            whole(256, 256),
+        ],
+        out_specs=(pl.BlockSpec((B, 256, 128), lambda i: (i, 0, 0)), whole(32, 224, 128)),
+        scratch_shapes=[
+            pltpu.VMEM((2, 256, 128), f32),
+            pltpu.VMEM((2, 128, 128), f32),
+            pltpu.VMEM((2, 8, 128), f32),
+        ],
+        compiler_params=pltpu.CompilerParams(vmem_limit_bytes=40 * 1024 * 1024),
+        cost_estimate=pl.CostEstimate(flops=4 * 10**9, bytes_accessed=7 * 2**20, transcendentals=0),
+        name="layers",
+    )(x, out_grad, wcol, wcol_t, expand_w, norm_gain, place)
 
 
 def shift_z(x, step):
@@ -42,7 +145,8 @@
     place = (feature_order[None, :] == jnp.arange(256, dtype=jnp.int32)[:, None]).astype(bf16)
     wcol = jnp.einsum("fj,lfk->ljk", place, compress_w, preferred_element_type=f32).astype(bf16)
     scaled = (pooled.astype(f32) * row_scale[:, :, None]).astype(bf16)
-    x_zero = lax.all_to_all(scaled, SHARD, split_axis=0, concat_axis=1, tiled=True)
+    wcol_t = jnp.einsum("fj,lfk->lkj", place, compress_w, preferred_element_type=f32).astype(bf16)
+    x_zero = lax.all_to_all(scaled, SHARD, split_axis=0, concat_axis=0, tiled=True).reshape(16, 24, 16, 128)
 
     marks = jnp.stack([row_ids.astype(f32), row_scale]).transpose(0, 2, 1).reshape(2, 2, 8, 384)
     mine = lax.dynamic_index_in_dim(marks, xl, 1, keepdims=False)
@@ -50,16 +154,7 @@
     low = xl == 0
     marks = jnp.concatenate([jnp.where(low, mine, other), jnp.where(low, other, mine)], axis=2)
 
-    features_out, pull = jax.vjp(layers, x_zero, wcol, expand_w, norm_gain)
-    grad_x, grad_w, grad_v, grad_g = pull(out_grad)
-    compress_part = jnp.einsum("fj,ljk->lfk", place, grad_w, preferred_element_type=f32).astype(bf16)
-    gain_high = grad_g.astype(bf16)
-    gain_low = (grad_g - gain_high.astype(f32)).astype(bf16)
-    dense = jnp.concatenate(
-        [compress_part.reshape(512, 128), grad_v.reshape(256, 128), gain_high, gain_low, jnp.zeros((252, 128), bf16)]
-    )
-    parcels = grad_x.reshape(24, 16, 2, 8, 128).transpose(2, 1, 0, 3, 4).reshape(32, 192, 128)
-    parcels = jnp.concatenate([parcels, dense.reshape(32, 32, 128)], axis=1)
+    features_out, parcels = run_layers(x_zero, out_grad, wcol, wcol_t, expand_w, norm_gain, place)
     parcels = lax.all_to_all(parcels, PLANE, split_axis=0, concat_axis=0, tiled=True)
 
     dense_part = jnp.sum(parcels[:, 192:].astype(f32), axis=0).astype(bf16)

time: 171 us -> 161 us (0.942)
  matrix products: 31.3 us -> 2.27 us
  Pallas kernels: 0 us -> 27 us
  other arithmetic: 9.37 us -> 4.06 us
  waiting for transfers between devices: 64.3 us -> 59.7 us
  starting transfers between devices: 28.3 us -> 32.6 us
  local copies, waits for them, and re-layouts: 8.39 us -> 6.31 us
    dot_general x19 -> x0, matrix products: 29 us -> none  [the longest x6 12.3 us: layers(): jnp.einsum('bfk,kd->bfd', inter, expand_w[layer], preferred_element_type=...]
    pallas_call x0 -> x1, Pallas kernels: none -> 27 us  [run_layers(): pl.pallas_call(layers_kernel, grid=(24 // B,), out_shape=(jax.ShapeDtypeS...]
    ppermute x8, starting transfers between devices: 9.04 us -> 13.1 us  [shift_z(): return lax.ppermute(x, 'z', [(i, (i + step) % 8) for i in range(8)])]
    ppermute x8, waiting for transfers between devices: 8.71 us -> 5.41 us  [shift_z(): return lax.ppermute(x, 'z', [(i, (i + step) % 8) for i in range(8)])]
    reduce_sum x1 -> x0, other arithmetic: 2.91 us -> none  [layers(): x = (mixed * scale * norm_gain[layer]).astype(jnp.bfloat16)]
    unnamed x23 -> x17, local copies, waits for them, and re-layouts: 3.48 us -> 3.65 us
where the time goes in v2:
time: 161 us; the launch traced here: 160 us
  waiting for transfers between devices  59.7 us (37%)
  starting transfers between devices  32.6 us (20%)
  blocking collectives  27.2 us (17%)
  Pallas kernels  27 us (17%)
  local copies, waits for them, and re-layouts  6.31 us (4%)
  other arithmetic  4.06 us (3%)
  matrix products  2.27 us (1%)
    all_to_all x1, blocking collectives, on_device(): lax.all_to_all(table_part, 'z', split_axis=0, concat_axis=0, tiled=True)  27.2 us
    pallas_call x1, Pallas kernels, run_layers(): pl.pallas_call(layers_kernel, grid=(24 // B,), out_shape=(jax.ShapeDtypeS...  27 us
    ppermute x2, waiting for transfers between devices, swap_xl(): return lax.ppermute(x, 'xl', [(0, 1), (1, 0)])  23.8 us
    all_to_all x1, waiting for transfers between devices, on_device(): lax.all_to_all(scaled, SHARD, split_axis=0, concat_axis=0, tiled=True)  23.3 us
    ppermute x8, starting transfers between devices, shift_z(): return lax.ppermute(x, 'z', [(i, (i + step) % 8) for i in range(8)])  13.1 us
    all_to_all x1, starting transfers between devices, on_device(): lax.all_to_all(scaled, SHARD, split_axis=0, concat_axis=0, tiled=True)  6.27 us
    all_to_all x1, starting transfers between devices, on_device(): lax.all_to_all(jnp.broadcast_to(dense_sum[None], (32, 32, 128)), PLANE, s...  5.9 us
    ppermute x8, waiting for transfers between devices, shift_z(): return lax.ppermute(x, 'z', [(i, (i + step) % 8) for i in range(8)])  5.41 us
  transfers between devices with their start and end apart: 13, of which 7 were waited for; matrix products, arithmetic and copies ran while one was open for 2% of the time, Pallas kernels for 0%

profile of v2, /device:TPU:2, one launch (start us, length us, event | category | flops | bytes accessed | tf_op | source)
XLA Modules:
  0.0 160.1 jit_solution(4825963761524436288)
XLA Ops:
  0.6 0.0 copy-start
  0.6 0.9 copy.13
  1.5 3.0 %multiply_convert_fusion = bf16[384,16,128]{2,1,0:T(8,128)(2,1)} fusion(bf16[384,16,128]{2,1,0:T(8,128)(2,1)} %param.8, f32[384,16]{1,0:T(8,128)S(1)} %copy.13), kind=kLoop, calls=%fused_computation.7 | loop fusion | flops 2359296 | bytes 3170304 | tf_op jit(solution)/shard_map/convert_element_type | solution.py:147
  4.5 0.0 copy-start.7
  4.5 0.0 copy-start.2
  4.5 0.0 copy-start.3
  4.5 6.3 %all-to-all-start = ((bf16[384,16,128]{2,1,0:T(8,128)(2,1)}), bf16[384,16,128]{2,1,0:T(8,128)(2,1)S(1)}, u32[]{:S(2)}, u32[]{:S(2)}) async-start(bf16[384,16,128]{2,1,0:T(8,128)(2,1)} %multiply_convert_fusion), calls=%async_computation | async-start | bytes 3145728 | tf_op jit(solution)/shard_map/all_to_all | solution.py:149
  10.8 0.0 copy-done
  10.8 0.0 copy-done.7
  10.8 0.2 convolution_convert_fusion
  11.1 0.1 copy.16.w_ref
  11.2 23.3 %all-to-all-done = bf16[384,16,128]{2,1,0:T(8,128)(2,1)S(1)} async-done(((bf16[384,16,128]{2,1,0:T(8,128)(2,1)}), bf16[384,16,128]{2,1,0:T(8,128)(2,1)S(1)}, u32[]{:S(2)}, u32[]{:S(2)}) %all-to-all-start) | async-done | bytes 1572896 | tf_op jit(solution)/shard_map/all_to_all | solution.py:149
  34.6 0.0 copy-done.2
  34.6 0.0 copy-done.3
  34.6 0.0 copy-start.1
  34.6 1.4 copy-done.1
  36.0 27.0 %layers.1 = (bf16[24,256,128]{2,1,0:T(8,128)(2,1)}, bf16[32,224,128]{2,1,0:T(8,128)(2,1)}) custom-call(bf16[16,24,16,128]{3,2,1,0:T(8,128)(2,1)S(1)} %bitcast.87, bf16[24,256,128]{2,1,0:T(8,128)(2,1)S(1)} %copy-done.1, bf16[2,256,128]{2,1,0:T(8,128)(2,1)S(1)} %copy.16.w_ref, bf16[2,128,256]{2,1,0:T(8,128)(2,1)S(1)} %bitcast.89, ...), custom_call_target="tpu_custom_call" | custom-call | flops 4000000000 | bytes 7340032 | tf_op jit(solution)/shard_map/layers/pallas_call | solution.py:105
  62.9 0.0 copy-start.6
  63.0 0.0 copy-start.5
  63.0 5.2 %all-to-all-start.1 = ((bf16[32,224,128]{2,1,0:T(8,128)(2,1)}), bf16[32,224,128]{2,1,0:T(8,128)(2,1)S(1)}, u32[]{:S(2)}, u32[]{:S(2)}) async-start(bf16[32,224,128]{2,1,0:T(8,128)(2,1)} %get-tuple-element.8), calls=%async_computation.1 | async-start | bytes 3670016 | tf_op jit(solution)/shard_map/all_to_all | solution.py:158
  68.2 0.0 copy-done.6
  68.2 0.0 copy-done.5
  68.3 0.3 collective-permute-start
  68.6 21.2 %collective-permute-done = f32[2,8,384]{2,1,0:T(8,128)S(1)} collective-permute-done((f32[2,8,384]{2,1,0:T(8,128)S(1)}, f32[2,8,384]{2,1,0:T(8,128)S(1)}, u32[]{:S(2)}, u32[]{:S(2)}) %collective-permute-start) | collective-permute-done | bytes 24608 | tf_op jit(solution)/shard_map/ppermute | solution.py:138
  89.8 2.9 %all-to-all-done.1 = bf16[32,224,128]{2,1,0:T(8,128)(2,1)S(1)} async-done(((bf16[32,224,128]{2,1,0:T(8,128)(2,1)}), bf16[32,224,128]{2,1,0:T(8,128)(2,1)S(1)}, u32[]{:S(2)}, u32[]{:S(2)}) %all-to-all-start.1) | async-done | bytes 1835040 | tf_op jit(solution)/shard_map/all_to_all | solution.py:158
  92.8 0.2 slice.53
  93.0 1.0 fusion.2
  94.0 1.0 fusion.19
  95.0 0.1 slice_reduce_fusion
  95.1 27.2 %all_to_all.20 = bf16[8,288,128]{2,1,0:T(8,128)(2,1)S(1)} all-to-all(bf16[8,288,128]{2,1,0:T(8,128)(2,1)S(1)} %pad_maximum_fusion), channel_id=1, replica_groups=mesh['z'=8,'xl'=2,'y'=4,'xh'=2,'core'=2] {'z'}, dimensions={0} | all-to-all | bytes 1179648 | tf_op jit(solution)/shard_map/all_to_all | solution.py:170
  122.3 0.1 reduce_sum.25
  122.4 1.7 %collective-permute-start.1 = (bf16[256,128]{1,0:T(8,128)(2,1)S(1)}, bf16[256,128]{1,0:T(8,128)(2,1)S(1)}, u32[]{:S(2)}, u32[]{:S(2)}) collective-permute-start(bf16[256,128]{1,0:T(8,128)(2,1)S(1)} %slice.55), channel_id=1, source_target_pairs={{0,16},{16,0},{1,17},{17,1},{2,18},{18,2},{3,19},{19,3},{4,20},{20... | collective-permute-start | bytes 196616 | tf_op jit(solution)/shard_map/ppermute | solution.py:138
  124.1 2.6 %collective-permute-done.1 = bf16[256,128]{1,0:T(8,128)(2,1)S(1)} collective-permute-done((bf16[256,128]{1,0:T(8,128)(2,1)S(1)}, bf16[256,128]{1,0:T(8,128)(2,1)S(1)}, u32[]{:S(2)}, u32[]{:S(2)}) %collective-permute-start.1) | collective-permute-done | bytes 65568 | tf_op jit(solution)/shard_map/ppermute | solution.py:138
  126.8 0.6 collective-permute-start.2
  127.5 2.7 %collective-permute-start.3 = (bf16[2,256,128]{2,1,0:T(8,128)(2,1)S(1)}, bf16[2,256,128]{2,1,0:T(8,128)(2,1)S(1)}, u32[]{:S(2)}, u32[]{:S(2)}) collective-permute-start(bf16[2,256,128]{2,1,0:T(8,128)(2,1)S(1)} %pad_maximum_fusion.1), channel_id=1, source_target_pairs={{0,224},{32,0},{64,32},{96,64},{128,96},{160,128},{192,160},{224,1... | collective-permute-start | bytes 393224 | tf_op jit(solution)/shard_map/ppermute | solution.py:134
  130.1 0.7 broadcast_in_dim.109
  130.9 5.9 %all-to-all-start.3 = ((bf16[32,32,128]{2,1,0:T(8,128)(2,1)}), bf16[32,32,128]{2,1,0:T(8,128)(2,1)S(1)}, u32[]{:S(2)}, u32[]{:S(2)}) async-start(bf16[32,32,128]{2,1,0:T(8,128)(2,1)} %broadcast_in_dim.109), calls=%async_computation.3 | async-start | bytes 524288 | tf_op jit(solution)/shard_map/all_to_all | solution.py:174
  136.8 0.2 broadcast_in_dim.88
  137.0 0.0 collective-permute-done.2
  137.0 0.1 collective-permute-start.4
  137.1 0.0 collective-permute-done.3
  137.1 3.2 %collective-permute-start.5 = (bf16[2,256,128]{2,1,0:T(8,128)(2,1)S(1)}, bf16[2,256,128]{2,1,0:T(8,128)(2,1)S(1)}, u32[]{:S(2)}, u32[]{:S(2)}) collective-permute-start(bf16[2,256,128]{2,1,0:T(8,128)(2,1)S(1)} %collective-permute-done.3), channel_id=1, source_target_pairs={{0,224},{32,0},{64,32},{96,64},{128,96},{160,128},{192,160},{224,1... | collective-permute-start | bytes 393224 | tf_op jit(solution)/shard_map/ppermute | solution.py:134
  140.4 4.2 %all-to-all-done.3 = bf16[32,32,128]{2,1,0:T(8,128)(2,1)S(1)} async-done(((bf16[32,32,128]{2,1,0:T(8,128)(2,1)}), bf16[32,32,128]{2,1,0:T(8,128)(2,1)S(1)}, u32[]{:S(2)}, u32[]{:S(2)}) %all-to-all-start.3) | async-done | bytes 262176 | tf_op jit(solution)/shard_map/all_to_all | solution.py:174
  144.7 0.7 slice.59
  145.4 0.7 slice.60
  146.1 0.6 slice_add_fusion
  146.6 0.0 collective-permute-done.4
  146.6 0.0 collective-permute-start.6
  146.6 0.0 collective-permute-done.5
  146.6 3.2 %collective-permute-start.7 = (bf16[2,256,128]{2,1,0:T(8,128)(2,1)S(1)}, bf16[2,256,128]{2,1,0:T(8,128)(2,1)S(1)}, u32[]{:S(2)}, u32[]{:S(2)}) collective-permute-start(bf16[2,256,128]{2,1,0:T(8,128)(2,1)S(1)} %collective-permute-done.5), channel_id=1, source_target_pairs={{0,224},{32,0},{64,32},{96,64},{128,96},{160,128},{192,160},{224,1... | collective-permute-start | bytes 393224 | tf_op jit(solution)/shard_map/ppermute | solution.py:134
  149.9 3.3 %collective-permute-done.6 = bf16[2,256,128]{2,1,0:T(8,128)(2,1)S(1)} collective-permute-done((bf16[2,256,128]{2,1,0:T(8,128)(2,1)S(1)}, bf16[2,256,128]{2,1,0:T(8,128)(2,1)S(1)}, u32[]{:S(2)}, u32[]{:S(2)}) %collective-permute-start.6) | collective-permute-done | bytes 131104 | tf_op jit(solution)/shard_map/ppermute | solution.py:134
  153.2 0.0 collective-permute-start.8
  153.2 0.0 collective-permute-done.7
  153.3 3.3 %collective-permute-start.9 = (bf16[2,128,128]{2,1,0:T(8,128)(2,1)S(1)}, bf16[2,128,128]{2,1,0:T(8,128)(2,1)S(1)}, u32[]{:S(2)}, u32[]{:S(2)}) collective-permute-start(bf16[2,128,128]{2,1,0:T(8,128)(2,1)S(1)} %slice.57), channel_id=1, source_target_pairs={{0,224},{32,0},{64,32},{96,64},{128,96},{160,128},{192,160},{224,1... | collective-permute-start | bytes 196616 | tf_op jit(solution)/shard_map/ppermute | solution.py:134
  156.6 2.1 %collective-permute-done.8 = bf16[2,128,128]{2,1,0:T(8,128)(2,1)S(1)} collective-permute-done((bf16[2,128,128]{2,1,0:T(8,128)(2,1)S(1)}, bf16[2,128,128]{2,1,0:T(8,128)(2,1)S(1)}, u32[]{:S(2)}, u32[]{:S(2)}) %collective-permute-start.8) | collective-permute-done | bytes 65568 | tf_op jit(solution)/shard_map/ppermute | solution.py:134
  158.7 0.0 collective-permute-done.9
  158.7 0.0 copy-start.4
  158.8 1.3 copy-done.4
  (26 shorter events, 0.4 us)
Async XLA Ops:
  0.6 10.2 %copy-start = (bf16[2,256,128]{2,1,0:T(8,128)(2,1)S(1)}, bf16[2,256,128]{2,1,0:T(8,128)(2,1)}, u32[]{:S(2)}) copy-start(bf16[2,256,128]{2,1,0:T(8,128)(2,1)} %param.12) | copy-start | bytes 393220
  4.5 6.3 %copy-start.7 = (s32[256]{0:T(256)S(1)}, s32[256]{0:T(256)}, u32[]{:S(2)}) copy-start(s32[256]{0:T(256)} %param.11) | copy-start | bytes 3076
  4.5 30.0 %copy-start.2 = (bf16[2,128,128]{2,1,0:T(8,128)(2,1)S(1)}, bf16[2,128,128]{2,1,0:T(8,128)(2,1)}, u32[]{:S(2)}) copy-start(bf16[2,128,128]{2,1,0:T(8,128)(2,1)} %v_ref.1) | copy-start | bytes 196612
  4.5 30.0 %copy-start.3 = (f32[2,128]{1,0:T(2,128)S(1)}, f32[2,128]{1,0:T(2,128)}, u32[]{:S(2)}) copy-start(f32[2,128]{1,0:T(2,128)} %gain_ref.1) | copy-start | bytes 3076
  4.5 30.0 %all-to-all-start = ((bf16[384,16,128]{2,1,0:T(8,128)(2,1)}), bf16[384,16,128]{2,1,0:T(8,128)(2,1)S(1)}, u32[]{:S(2)}, u32[]{:S(2)}) async-start(bf16[384,16,128]{2,1,0:T(8,128)(2,1)} %multiply_convert_fusion), calls=%async_computation | async-start | bytes 3145728 | tf_op jit(solution)/shard_map/all_to_all | solution.py:149
  34.6 1.4 copy-start.1
  62.9 5.3 %copy-start.6 = (s32[384,16]{0,1:T(8,128)S(1)}, s32[384,16]{0,1:T(8,128)}, u32[]{:S(2)}) copy-start(s32[384,16]{0,1:T(8,128)} %param.10) | copy-start | bytes 73732
  63.0 5.3 %copy-start.5 = (f32[384,16]{0,1:T(8,128)S(1)}, f32[384,16]{0,1:T(8,128)}, u32[]{:S(2)}) copy-start(f32[384,16]{0,1:T(8,128)} %param.9) | copy-start | bytes 73732
  63.0 29.8 %all-to-all-start.1 = ((bf16[32,224,128]{2,1,0:T(8,128)(2,1)}), bf16[32,224,128]{2,1,0:T(8,128)(2,1)S(1)}, u32[]{:S(2)}, u32[]{:S(2)}) async-start(bf16[32,224,128]{2,1,0:T(8,128)(2,1)} %get-tuple-element.8), calls=%async_computation.1 | async-start | bytes 3670016 | tf_op jit(solution)/shard_map/all_to_all | solution.py:158
  68.3 21.5 %collective-permute-start = (f32[2,8,384]{2,1,0:T(8,128)S(1)}, f32[2,8,384]{2,1,0:T(8,128)S(1)}, u32[]{:S(2)}, u32[]{:S(2)}) collective-permute-start(f32[2,8,384]{2,1,0:T(8,128)S(1)} %dynamic-slice_bitcast_fusion), channel_id=1, source_target_pairs={{0,16},{16,0},{1,17},{17,1},{2,18},{18,2},{3,19},{19,3},{4,20},{20... | collective-permute-start | bytes 73736 | tf_op jit(solution)/shard_map/ppermute | solution.py:138
  122.4 4.4 %collective-permute-start.1 = (bf16[256,128]{1,0:T(8,128)(2,1)S(1)}, bf16[256,128]{1,0:T(8,128)(2,1)S(1)}, u32[]{:S(2)}, u32[]{:S(2)}) collective-permute-start(bf16[256,128]{1,0:T(8,128)(2,1)S(1)} %slice.55), channel_id=1, source_target_pairs={{0,16},{16,0},{1,17},{17,1},{2,18},{18,2},{3,19},{19,3},{4,20},{20... | collective-permute-start | bytes 196616 | tf_op jit(solution)/shard_map/ppermute | solution.py:138
  126.8 10.2 %collective-permute-start.2 = (bf16[2,256,128]{2,1,0:T(8,128)(2,1)S(1)}, bf16[2,256,128]{2,1,0:T(8,128)(2,1)S(1)}, u32[]{:S(2)}, u32[]{:S(2)}) collective-permute-start(bf16[2,256,128]{2,1,0:T(8,128)(2,1)S(1)} %pad_maximum_fusion.1), channel_id=1, source_target_pairs={{0,32},{32,64},{64,96},{96,128},{128,160},{160,192},{192,224},{224... | collective-permute-start | bytes 393224 | tf_op jit(solution)/shard_map/ppermute | solution.py:134
  127.5 9.7 %collective-permute-start.3 = (bf16[2,256,128]{2,1,0:T(8,128)(2,1)S(1)}, bf16[2,256,128]{2,1,0:T(8,128)(2,1)S(1)}, u32[]{:S(2)}, u32[]{:S(2)}) collective-permute-start(bf16[2,256,128]{2,1,0:T(8,128)(2,1)S(1)} %pad_maximum_fusion.1), channel_id=1, source_target_pairs={{0,224},{32,0},{64,32},{96,64},{128,96},{160,128},{192,160},{224,1... | collective-permute-start | bytes 393224 | tf_op jit(solution)/shard_map/ppermute | solution.py:134
  130.9 13.7 %all-to-all-start.3 = ((bf16[32,32,128]{2,1,0:T(8,128)(2,1)}), bf16[32,32,128]{2,1,0:T(8,128)(2,1)S(1)}, u32[]{:S(2)}, u32[]{:S(2)}) async-start(bf16[32,32,128]{2,1,0:T(8,128)(2,1)} %broadcast_in_dim.109), calls=%async_computation.3 | async-start | bytes 524288 | tf_op jit(solution)/shard_map/all_to_all | solution.py:174
  137.0 9.6 %collective-permute-start.4 = (bf16[2,256,128]{2,1,0:T(8,128)(2,1)S(1)}, bf16[2,256,128]{2,1,0:T(8,128)(2,1)S(1)}, u32[]{:S(2)}, u32[]{:S(2)}) collective-permute-start(bf16[2,256,128]{2,1,0:T(8,128)(2,1)S(1)} %collective-permute-done.2), channel_id=1, source_target_pairs={{0,32},{32,64},{64,96},{96,128},{128,160},{160,192},{192,224},{224... | collective-permute-start | bytes 393224 | tf_op jit(solution)/shard_map/ppermute | solution.py:134
  137.1 9.5 %collective-permute-start.5 = (bf16[2,256,128]{2,1,0:T(8,128)(2,1)S(1)}, bf16[2,256,128]{2,1,0:T(8,128)(2,1)S(1)}, u32[]{:S(2)}, u32[]{:S(2)}) collective-permute-start(bf16[2,256,128]{2,1,0:T(8,128)(2,1)S(1)} %collective-permute-done.3), channel_id=1, source_target_pairs={{0,224},{32,0},{64,32},{96,64},{128,96},{160,128},{192,160},{224,1... | collective-permute-start | bytes 393224 | tf_op jit(solution)/shard_map/ppermute | solution.py:134
  146.6 6.6 %collective-permute-start.6 = (bf16[2,256,128]{2,1,0:T(8,128)(2,1)S(1)}, bf16[2,256,128]{2,1,0:T(8,128)(2,1)S(1)}, u32[]{:S(2)}, u32[]{:S(2)}) collective-permute-start(bf16[2,256,128]{2,1,0:T(8,128)(2,1)S(1)} %collective-permute-done.4), channel_id=1, source_target_pairs={{0,32},{32,64},{64,96},{96,128},{128,160},{160,192},{192,224},{224... | collective-permute-start | bytes 393224 | tf_op jit(solution)/shard_map/ppermute | solution.py:134
  146.6 6.6 %collective-permute-start.7 = (bf16[2,256,128]{2,1,0:T(8,128)(2,1)S(1)}, bf16[2,256,128]{2,1,0:T(8,128)(2,1)S(1)}, u32[]{:S(2)}, u32[]{:S(2)}) collective-permute-start(bf16[2,256,128]{2,1,0:T(8,128)(2,1)S(1)} %collective-permute-done.5), channel_id=1, source_target_pairs={{0,224},{32,0},{64,32},{96,64},{128,96},{160,128},{192,160},{224,1... | collective-permute-start | bytes 393224 | tf_op jit(solution)/shard_map/ppermute | solution.py:134
  153.2 5.5 %collective-permute-start.8 = (bf16[2,128,128]{2,1,0:T(8,128)(2,1)S(1)}, bf16[2,128,128]{2,1,0:T(8,128)(2,1)S(1)}, u32[]{:S(2)}, u32[]{:S(2)}) collective-permute-start(bf16[2,128,128]{2,1,0:T(8,128)(2,1)S(1)} %slice.56), channel_id=1, source_target_pairs={{0,32},{32,64},{64,96},{96,128},{128,160},{160,192},{192,224},{224... | collective-permute-start | bytes 196616 | tf_op jit(solution)/shard_map/ppermute | solution.py:134
  153.3 5.5 %collective-permute-start.9 = (bf16[2,128,128]{2,1,0:T(8,128)(2,1)S(1)}, bf16[2,128,128]{2,1,0:T(8,128)(2,1)S(1)}, u32[]{:S(2)}, u32[]{:S(2)}) collective-permute-start(bf16[2,128,128]{2,1,0:T(8,128)(2,1)S(1)} %slice.57), channel_id=1, source_target_pairs={{0,224},{32,0},{64,32},{96,64},{128,96},{160,128},{192,160},{224,1... | collective-permute-start | bytes 196616 | tf_op jit(solution)/shard_map/ppermute | solution.py:134
  158.7 1.3 copy-start.4

commit v3 on v2

--- a/solution.py
+++ b/solution.py
@@ -18,7 +18,8 @@
 
 NT = ((1,), (1,))
 TN = ((0,), (0,))
-B = 4
+B = 12
+G = 6
 
 
 def layers_kernel(x_ref, og_ref, w_ref, wt_ref, v_ref, gain_ref, place_ref, feat_ref, out_ref, dw, dv, dg):
@@ -58,21 +59,28 @@
         dw_sum = 0.0
         dv_sum = 0.0
         dg_sum = 0.0
-        for b in range(B):
-            n, r = kept[b]
-            cn = c[b] * n
-            dg_sum = dg_sum + jnp.sum(cn.reshape(32, 8, 128), axis=0)
-            mean = jnp.mean(cn * gain, axis=-1, keepdims=True)
-            dz = r * (c[b] * gain - n * mean)
-            dzb = dz.astype(bf16)
-            dv_sum = dv_sum + dot(inter[b], dzb, TN)
-            dint = dot(dzb, v_ref[layer], NT).astype(bf16)
-            dut = dot(dint, x[b], TN).astype(bf16)
-            left = jnp.concatenate([dint, w_ref[layer]], axis=1)
-            right = jnp.concatenate([ut[b], dut], axis=0)
-            dx = (dz + dot(left, right) * root).astype(bf16)
-            dw_sum = dw_sum + dot(x[b], dut, NT)
-            below.append(dx.astype(f32))
+        for start in range(0, B, G):
+            group = range(start, start + G)
+            dz, dzb, dint, dut = {}, {}, {}, {}
+            for b in group:
+                n, r = kept[b]
+                cn = c[b] * n
+                dg_sum = dg_sum + jnp.sum(cn.reshape(32, 8, 128), axis=0)
+                mean = jnp.mean(cn * gain, axis=-1, keepdims=True)
+                dz[b] = r * (c[b] * gain - n * mean)
+                dzb[b] = dz[b].astype(bf16)
+            for b in group:
+                dint[b] = dot(dzb[b], v_ref[layer], NT).astype(bf16)
+            for b in group:
+                dv_sum = dv_sum + dot(inter[b], dzb[b], TN)
+            for b in group:
+                dut[b] = dot(dint[b], x[b], TN).astype(bf16)
+            for b in group:
+                left = jnp.concatenate([dint[b], w_ref[layer]], axis=1)
+                right = jnp.concatenate([ut[b], dut[b]], axis=0)
+                below.append((dz[b] + dot(left, right) * root).astype(bf16).astype(f32))
+            for b in group:
+                dw_sum = dw_sum + dot(x[b], dut[b], NT)
         dw[layer] += dw_sum
         dv[layer] += dv_sum
         dg[layer] += dg_sum

time: 161 us -> 146 us (0.907)
  Pallas kernels: 27 us -> 12.3 us
    pallas_call x1, Pallas kernels: 27 us -> 12.3 us  [run_layers(): pl.pallas_call(layers_kernel, grid=(24 // B,), out_shape=(jax.ShapeDtypeS...]
where the time goes in v3:
time: 146 us; the launch traced here: 145 us
  waiting for transfers between devices  59.7 us (41%)
  starting transfers between devices  32.6 us (22%)
  blocking collectives  27.2 us (19%)
  Pallas kernels  12.3 us (8%)
  local copies, waits for them, and re-layouts  6.31 us (4%)
  other arithmetic  4.06 us (3%)
  matrix products  2.27 us (2%)
    all_to_all x1, blocking collectives, on_device(): lax.all_to_all(table_part, 'z', split_axis=0, concat_axis=0, tiled=True)  27.2 us
    ppermute x2, waiting for transfers between devices, swap_xl(): return lax.ppermute(x, 'xl', [(0, 1), (1, 0)])  23.8 us
    all_to_all x1, waiting for transfers between devices, on_device(): lax.all_to_all(scaled, SHARD, split_axis=0, concat_axis=0, tiled=True)  23.3 us
    ppermute x8, starting transfers between devices, shift_z(): return lax.ppermute(x, 'z', [(i, (i + step) % 8) for i in range(8)])  13.1 us
    pallas_call x1, Pallas kernels, run_layers(): pl.pallas_call(layers_kernel, grid=(24 // B,), out_shape=(jax.ShapeDtypeS...  12.3 us
    all_to_all x1, starting transfers between devices, on_device(): lax.all_to_all(scaled, SHARD, split_axis=0, concat_axis=0, tiled=True)  6.27 us
    all_to_all x1, starting transfers between devices, on_device(): lax.all_to_all(jnp.broadcast_to(dense_sum[None], (32, 32, 128)), PLANE, s...  5.9 us
    ppermute x8, waiting for transfers between devices, shift_z(): return lax.ppermute(x, 'z', [(i, (i + step) % 8) for i in range(8)])  5.41 us
  transfers between devices with their start and end apart: 13, of which 7 were waited for; matrix products, arithmetic and copies ran while one was open for 2% of the time, Pallas kernels for 0%

profile of v3, /device:TPU:2, one launch (start us, length us, event | category | flops | bytes accessed | tf_op | source)
XLA Modules:
  0.0 145.4 jit_solution(13108083416556119268)
XLA Ops:
  0.6 0.0 copy-start
  0.6 0.9 copy.13
  1.5 3.0 %multiply_convert_fusion = bf16[384,16,128]{2,1,0:T(8,128)(2,1)} fusion(bf16[384,16,128]{2,1,0:T(8,128)(2,1)} %param.8, f32[384,16]{1,0:T(8,128)S(1)} %copy.13), kind=kLoop, calls=%fused_computation.7 | loop fusion | flops 2359296 | bytes 3170304 | tf_op jit(solution)/shard_map/convert_element_type | solution.py:155
  4.5 0.0 copy-start.7
  4.5 0.0 copy-start.2
  4.5 0.0 copy-start.3
  4.5 6.3 %all-to-all-start = ((bf16[384,16,128]{2,1,0:T(8,128)(2,1)}), bf16[384,16,128]{2,1,0:T(8,128)(2,1)S(1)}, u32[]{:S(2)}, u32[]{:S(2)}) async-start(bf16[384,16,128]{2,1,0:T(8,128)(2,1)} %multiply_convert_fusion), calls=%async_computation | async-start | bytes 3145728 | tf_op jit(solution)/shard_map/all_to_all | solution.py:157
  10.8 0.0 copy-done
  10.8 0.0 copy-done.7
  10.8 0.2 convolution_convert_fusion
  11.1 0.1 copy.16.w_ref
  11.2 23.3 %all-to-all-done = bf16[384,16,128]{2,1,0:T(8,128)(2,1)S(1)} async-done(((bf16[384,16,128]{2,1,0:T(8,128)(2,1)}), bf16[384,16,128]{2,1,0:T(8,128)(2,1)S(1)}, u32[]{:S(2)}, u32[]{:S(2)}) %all-to-all-start) | async-done | bytes 1572896 | tf_op jit(solution)/shard_map/all_to_all | solution.py:157
  34.6 0.0 copy-done.2
  34.6 0.0 copy-done.3
  34.6 0.0 copy-start.1
  34.6 1.4 copy-done.1
  36.0 12.3 %layers.1 = (bf16[24,256,128]{2,1,0:T(8,128)(2,1)}, bf16[32,224,128]{2,1,0:T(8,128)(2,1)}) custom-call(bf16[16,24,16,128]{3,2,1,0:T(8,128)(2,1)S(1)} %bitcast.87, bf16[24,256,128]{2,1,0:T(8,128)(2,1)S(1)} %copy-done.1, bf16[2,256,128]{2,1,0:T(8,128)(2,1)S(1)} %copy.16.w_ref, bf16[2,128,256]{2,1,0:T(8,128)(2,1)S(1)} %bitcast.89, ...), custom_call_target="tpu_custom_call" | custom-call | flops 4000000000 | bytes 7340032 | tf_op jit(solution)/shard_map/layers/pallas_call | solution.py:113
  48.3 0.0 copy-start.6
  48.3 0.0 copy-start.5
  48.3 5.3 %all-to-all-start.1 = ((bf16[32,224,128]{2,1,0:T(8,128)(2,1)}), bf16[32,224,128]{2,1,0:T(8,128)(2,1)S(1)}, u32[]{:S(2)}, u32[]{:S(2)}) async-start(bf16[32,224,128]{2,1,0:T(8,128)(2,1)} %get-tuple-element.8), calls=%async_computation.1 | async-start | bytes 3670016 | tf_op jit(solution)/shard_map/all_to_all | solution.py:166
  53.6 0.0 copy-done.6
  53.6 0.0 copy-done.5
  53.6 0.3 collective-permute-start
  54.0 21.2 %collective-permute-done = f32[2,8,384]{2,1,0:T(8,128)S(1)} collective-permute-done((f32[2,8,384]{2,1,0:T(8,128)S(1)}, f32[2,8,384]{2,1,0:T(8,128)S(1)}, u32[]{:S(2)}, u32[]{:S(2)}) %collective-permute-start) | collective-permute-done | bytes 24608 | tf_op jit(solution)/shard_map/ppermute | solution.py:146
  75.2 2.9 %all-to-all-done.1 = bf16[32,224,128]{2,1,0:T(8,128)(2,1)S(1)} async-done(((bf16[32,224,128]{2,1,0:T(8,128)(2,1)}), bf16[32,224,128]{2,1,0:T(8,128)(2,1)S(1)}, u32[]{:S(2)}, u32[]{:S(2)}) %all-to-all-start.1) | async-done | bytes 1835040 | tf_op jit(solution)/shard_map/all_to_all | solution.py:166
  78.2 0.2 slice.53
  78.3 1.0 fusion.2
  79.3 1.0 fusion.19
  80.4 0.1 slice_reduce_fusion
  80.5 27.2 %all_to_all.20 = bf16[8,288,128]{2,1,0:T(8,128)(2,1)S(1)} all-to-all(bf16[8,288,128]{2,1,0:T(8,128)(2,1)S(1)} %pad_maximum_fusion), channel_id=1, replica_groups=mesh['z'=8,'xl'=2,'y'=4,'xh'=2,'core'=2] {'z'}, dimensions={0} | all-to-all | bytes 1179648 | tf_op jit(solution)/shard_map/all_to_all | solution.py:178
  107.7 0.1 reduce_sum.25
  107.8 1.7 %collective-permute-start.1 = (bf16[256,128]{1,0:T(8,128)(2,1)S(1)}, bf16[256,128]{1,0:T(8,128)(2,1)S(1)}, u32[]{:S(2)}, u32[]{:S(2)}) collective-permute-start(bf16[256,128]{1,0:T(8,128)(2,1)S(1)} %slice.55), channel_id=1, source_target_pairs={{0,16},{16,0},{1,17},{17,1},{2,18},{18,2},{3,19},{19,3},{4,20},{20... | collective-permute-start | bytes 196616 | tf_op jit(solution)/shard_map/ppermute | solution.py:146
  109.5 2.6 %collective-permute-done.1 = bf16[256,128]{1,0:T(8,128)(2,1)S(1)} collective-permute-done((bf16[256,128]{1,0:T(8,128)(2,1)S(1)}, bf16[256,128]{1,0:T(8,128)(2,1)S(1)}, u32[]{:S(2)}, u32[]{:S(2)}) %collective-permute-start.1) | collective-permute-done | bytes 65568 | tf_op jit(solution)/shard_map/ppermute | solution.py:146
  112.2 0.6 collective-permute-start.2
  112.8 2.7 %collective-permute-start.3 = (bf16[2,256,128]{2,1,0:T(8,128)(2,1)S(1)}, bf16[2,256,128]{2,1,0:T(8,128)(2,1)S(1)}, u32[]{:S(2)}, u32[]{:S(2)}) collective-permute-start(bf16[2,256,128]{2,1,0:T(8,128)(2,1)S(1)} %pad_maximum_fusion.1), channel_id=1, source_target_pairs={{0,224},{32,0},{64,32},{96,64},{128,96},{160,128},{192,160},{224,1... | collective-permute-start | bytes 393224 | tf_op jit(solution)/shard_map/ppermute | solution.py:142
  115.5 0.7 broadcast_in_dim.109
  116.2 5.9 %all-to-all-start.3 = ((bf16[32,32,128]{2,1,0:T(8,128)(2,1)}), bf16[32,32,128]{2,1,0:T(8,128)(2,1)S(1)}, u32[]{:S(2)}, u32[]{:S(2)}) async-start(bf16[32,32,128]{2,1,0:T(8,128)(2,1)} %broadcast_in_dim.109), calls=%async_computation.3 | async-start | bytes 524288 | tf_op jit(solution)/shard_map/all_to_all | solution.py:182
  122.1 0.2 broadcast_in_dim.88
  122.4 0.0 collective-permute-done.2
  122.4 0.1 collective-permute-start.4
  122.5 0.0 collective-permute-done.3
  122.5 3.2 %collective-permute-start.5 = (bf16[2,256,128]{2,1,0:T(8,128)(2,1)S(1)}, bf16[2,256,128]{2,1,0:T(8,128)(2,1)S(1)}, u32[]{:S(2)}, u32[]{:S(2)}) collective-permute-start(bf16[2,256,128]{2,1,0:T(8,128)(2,1)S(1)} %collective-permute-done.3), channel_id=1, source_target_pairs={{0,224},{32,0},{64,32},{96,64},{128,96},{160,128},{192,160},{224,1... | collective-permute-start | bytes 393224 | tf_op jit(solution)/shard_map/ppermute | solution.py:142
  125.8 4.2 %all-to-all-done.3 = bf16[32,32,128]{2,1,0:T(8,128)(2,1)S(1)} async-done(((bf16[32,32,128]{2,1,0:T(8,128)(2,1)}), bf16[32,32,128]{2,1,0:T(8,128)(2,1)S(1)}, u32[]{:S(2)}, u32[]{:S(2)}) %all-to-all-start.3) | async-done | bytes 262176 | tf_op jit(solution)/shard_map/all_to_all | solution.py:182
  130.0 0.7 slice.59
  130.7 0.7 slice.60
  131.4 0.6 slice_add_fusion
  132.0 0.0 collective-permute-done.4
  132.0 0.0 collective-permute-start.6
  132.0 0.0 collective-permute-done.5
  132.0 3.2 %collective-permute-start.7 = (bf16[2,256,128]{2,1,0:T(8,128)(2,1)S(1)}, bf16[2,256,128]{2,1,0:T(8,128)(2,1)S(1)}, u32[]{:S(2)}, u32[]{:S(2)}) collective-permute-start(bf16[2,256,128]{2,1,0:T(8,128)(2,1)S(1)} %collective-permute-done.5), channel_id=1, source_target_pairs={{0,224},{32,0},{64,32},{96,64},{128,96},{160,128},{192,160},{224,1... | collective-permute-start | bytes 393224 | tf_op jit(solution)/shard_map/ppermute | solution.py:142
  135.3 3.3 %collective-permute-done.6 = bf16[2,256,128]{2,1,0:T(8,128)(2,1)S(1)} collective-permute-done((bf16[2,256,128]{2,1,0:T(8,128)(2,1)S(1)}, bf16[2,256,128]{2,1,0:T(8,128)(2,1)S(1)}, u32[]{:S(2)}, u32[]{:S(2)}) %collective-permute-start.6) | collective-permute-done | bytes 131104 | tf_op jit(solution)/shard_map/ppermute | solution.py:142
  138.6 0.0 collective-permute-start.8
  138.6 0.0 collective-permute-done.7
  138.6 3.3 %collective-permute-start.9 = (bf16[2,128,128]{2,1,0:T(8,128)(2,1)S(1)}, bf16[2,128,128]{2,1,0:T(8,128)(2,1)S(1)}, u32[]{:S(2)}, u32[]{:S(2)}) collective-permute-start(bf16[2,128,128]{2,1,0:T(8,128)(2,1)S(1)} %slice.57), channel_id=1, source_target_pairs={{0,224},{32,0},{64,32},{96,64},{128,96},{160,128},{192,160},{224,1... | collective-permute-start | bytes 196616 | tf_op jit(solution)/shard_map/ppermute | solution.py:142
  142.0 2.1 %collective-permute-done.8 = bf16[2,128,128]{2,1,0:T(8,128)(2,1)S(1)} collective-permute-done((bf16[2,128,128]{2,1,0:T(8,128)(2,1)S(1)}, bf16[2,128,128]{2,1,0:T(8,128)(2,1)S(1)}, u32[]{:S(2)}, u32[]{:S(2)}) %collective-permute-start.8) | collective-permute-done | bytes 65568 | tf_op jit(solution)/shard_map/ppermute | solution.py:142
  144.1 0.0 collective-permute-done.9
  144.1 0.0 copy-start.4
  144.1 1.3 copy-done.4
  (26 shorter events, 0.4 us)
Async XLA Ops:
  0.6 10.2 %copy-start = (bf16[2,256,128]{2,1,0:T(8,128)(2,1)S(1)}, bf16[2,256,128]{2,1,0:T(8,128)(2,1)}, u32[]{:S(2)}) copy-start(bf16[2,256,128]{2,1,0:T(8,128)(2,1)} %param.12) | copy-start | bytes 393220
  4.5 6.3 %copy-start.7 = (s32[256]{0:T(256)S(1)}, s32[256]{0:T(256)}, u32[]{:S(2)}) copy-start(s32[256]{0:T(256)} %param.11) | copy-start | bytes 3076
  4.5 30.0 %copy-start.2 = (bf16[2,128,128]{2,1,0:T(8,128)(2,1)S(1)}, bf16[2,128,128]{2,1,0:T(8,128)(2,1)}, u32[]{:S(2)}) copy-start(bf16[2,128,128]{2,1,0:T(8,128)(2,1)} %v_ref.1) | copy-start | bytes 196612
  4.5 30.0 %copy-start.3 = (f32[2,128]{1,0:T(2,128)S(1)}, f32[2,128]{1,0:T(2,128)}, u32[]{:S(2)}) copy-start(f32[2,128]{1,0:T(2,128)} %gain_ref.1) | copy-start | bytes 3076
  4.5 30.0 %all-to-all-start = ((bf16[384,16,128]{2,1,0:T(8,128)(2,1)}), bf16[384,16,128]{2,1,0:T(8,128)(2,1)S(1)}, u32[]{:S(2)}, u32[]{:S(2)}) async-start(bf16[384,16,128]{2,1,0:T(8,128)(2,1)} %multiply_convert_fusion), calls=%async_computation | async-start | bytes 3145728 | tf_op jit(solution)/shard_map/all_to_all | solution.py:157
  34.6 1.4 copy-start.1
  48.3 5.3 %copy-start.6 = (s32[384,16]{0,1:T(8,128)S(1)}, s32[384,16]{0,1:T(8,128)}, u32[]{:S(2)}) copy-start(s32[384,16]{0,1:T(8,128)} %param.10) | copy-start | bytes 73732
  48.3 5.3 %copy-start.5 = (f32[384,16]{0,1:T(8,128)S(1)}, f32[384,16]{0,1:T(8,128)}, u32[]{:S(2)}) copy-start(f32[384,16]{0,1:T(8,128)} %param.9) | copy-start | bytes 73732
  48.3 29.8 %all-to-all-start.1 = ((bf16[32,224,128]{2,1,0:T(8,128)(2,1)}), bf16[32,224,128]{2,1,0:T(8,128)(2,1)S(1)}, u32[]{:S(2)}, u32[]{:S(2)}) async-start(bf16[32,224,128]{2,1,0:T(8,128)(2,1)} %get-tuple-element.8), calls=%async_computation.1 | async-start | bytes 3670016 | tf_op jit(solution)/shard_map/all_to_all | solution.py:166
  53.6 21.5 %collective-permute-start = (f32[2,8,384]{2,1,0:T(8,128)S(1)}, f32[2,8,384]{2,1,0:T(8,128)S(1)}, u32[]{:S(2)}, u32[]{:S(2)}) collective-permute-start(f32[2,8,384]{2,1,0:T(8,128)S(1)} %dynamic-slice_bitcast_fusion), channel_id=1, source_target_pairs={{0,16},{16,0},{1,17},{17,1},{2,18},{18,2},{3,19},{19,3},{4,20},{20... | collective-permute-start | bytes 73736 | tf_op jit(solution)/shard_map/ppermute | solution.py:146
  107.8 4.4 %collective-permute-start.1 = (bf16[256,128]{1,0:T(8,128)(2,1)S(1)}, bf16[256,128]{1,0:T(8,128)(2,1)S(1)}, u32[]{:S(2)}, u32[]{:S(2)}) collective-permute-start(bf16[256,128]{1,0:T(8,128)(2,1)S(1)} %slice.55), channel_id=1, source_target_pairs={{0,16},{16,0},{1,17},{17,1},{2,18},{18,2},{3,19},{19,3},{4,20},{20... | collective-permute-start | bytes 196616 | tf_op jit(solution)/shard_map/ppermute | solution.py:146
  112.2 10.2 %collective-permute-start.2 = (bf16[2,256,128]{2,1,0:T(8,128)(2,1)S(1)}, bf16[2,256,128]{2,1,0:T(8,128)(2,1)S(1)}, u32[]{:S(2)}, u32[]{:S(2)}) collective-permute-start(bf16[2,256,128]{2,1,0:T(8,128)(2,1)S(1)} %pad_maximum_fusion.1), channel_id=1, source_target_pairs={{0,32},{32,64},{64,96},{96,128},{128,160},{160,192},{192,224},{224... | collective-permute-start | bytes 393224 | tf_op jit(solution)/shard_map/ppermute | solution.py:142
  112.8 9.7 %collective-permute-start.3 = (bf16[2,256,128]{2,1,0:T(8,128)(2,1)S(1)}, bf16[2,256,128]{2,1,0:T(8,128)(2,1)S(1)}, u32[]{:S(2)}, u32[]{:S(2)}) collective-permute-start(bf16[2,256,128]{2,1,0:T(8,128)(2,1)S(1)} %pad_maximum_fusion.1), channel_id=1, source_target_pairs={{0,224},{32,0},{64,32},{96,64},{128,96},{160,128},{192,160},{224,1... | collective-permute-start | bytes 393224 | tf_op jit(solution)/shard_map/ppermute | solution.py:142
  116.2 13.7 %all-to-all-start.3 = ((bf16[32,32,128]{2,1,0:T(8,128)(2,1)}), bf16[32,32,128]{2,1,0:T(8,128)(2,1)S(1)}, u32[]{:S(2)}, u32[]{:S(2)}) async-start(bf16[32,32,128]{2,1,0:T(8,128)(2,1)} %broadcast_in_dim.109), calls=%async_computation.3 | async-start | bytes 524288 | tf_op jit(solution)/shard_map/all_to_all | solution.py:182
  122.4 9.6 %collective-permute-start.4 = (bf16[2,256,128]{2,1,0:T(8,128)(2,1)S(1)}, bf16[2,256,128]{2,1,0:T(8,128)(2,1)S(1)}, u32[]{:S(2)}, u32[]{:S(2)}) collective-permute-start(bf16[2,256,128]{2,1,0:T(8,128)(2,1)S(1)} %collective-permute-done.2), channel_id=1, source_target_pairs={{0,32},{32,64},{64,96},{96,128},{128,160},{160,192},{192,224},{224... | collective-permute-start | bytes 393224 | tf_op jit(solution)/shard_map/ppermute | solution.py:142
  122.5 9.5 %collective-permute-start.5 = (bf16[2,256,128]{2,1,0:T(8,128)(2,1)S(1)}, bf16[2,256,128]{2,1,0:T(8,128)(2,1)S(1)}, u32[]{:S(2)}, u32[]{:S(2)}) collective-permute-start(bf16[2,256,128]{2,1,0:T(8,128)(2,1)S(1)} %collective-permute-done.3), channel_id=1, source_target_pairs={{0,224},{32,0},{64,32},{96,64},{128,96},{160,128},{192,160},{224,1... | collective-permute-start | bytes 393224 | tf_op jit(solution)/shard_map/ppermute | solution.py:142
  132.0 6.6 %collective-permute-start.6 = (bf16[2,256,128]{2,1,0:T(8,128)(2,1)S(1)}, bf16[2,256,128]{2,1,0:T(8,128)(2,1)S(1)}, u32[]{:S(2)}, u32[]{:S(2)}) collective-permute-start(bf16[2,256,128]{2,1,0:T(8,128)(2,1)S(1)} %collective-permute-done.4), channel_id=1, source_target_pairs={{0,32},{32,64},{64,96},{96,128},{128,160},{160,192},{192,224},{224... | collective-permute-start | bytes 393224 | tf_op jit(solution)/shard_map/ppermute | solution.py:142
  132.0 6.6 %collective-permute-start.7 = (bf16[2,256,128]{2,1,0:T(8,128)(2,1)S(1)}, bf16[2,256,128]{2,1,0:T(8,128)(2,1)S(1)}, u32[]{:S(2)}, u32[]{:S(2)}) collective-permute-start(bf16[2,256,128]{2,1,0:T(8,128)(2,1)S(1)} %collective-permute-done.5), channel_id=1, source_target_pairs={{0,224},{32,0},{64,32},{96,64},{128,96},{160,128},{192,160},{224,1... | collective-permute-start | bytes 393224 | tf_op jit(solution)/shard_map/ppermute | solution.py:142
  138.6 5.5 %collective-permute-start.8 = (bf16[2,128,128]{2,1,0:T(8,128)(2,1)S(1)}, bf16[2,128,128]{2,1,0:T(8,128)(2,1)S(1)}, u32[]{:S(2)}, u32[]{:S(2)}) collective-permute-start(bf16[2,128,128]{2,1,0:T(8,128)(2,1)S(1)} %slice.56), channel_id=1, source_target_pairs={{0,32},{32,64},{64,96},{96,128},{128,160},{160,192},{192,224},{224... | collective-permute-start | bytes 196616 | tf_op jit(solution)/shard_map/ppermute | solution.py:142
  138.6 5.5 %collective-permute-start.9 = (bf16[2,128,128]{2,1,0:T(8,128)(2,1)S(1)}, bf16[2,128,128]{2,1,0:T(8,128)(2,1)S(1)}, u32[]{:S(2)}, u32[]{:S(2)}) collective-permute-start(bf16[2,128,128]{2,1,0:T(8,128)(2,1)S(1)} %slice.57), channel_id=1, source_target_pairs={{0,224},{32,0},{64,32},{96,64},{128,96},{160,128},{192,160},{224,1... | collective-permute-start | bytes 196616 | tf_op jit(solution)/shard_map/ppermute | solution.py:142
  144.1 1.3 copy-start.4

commit v4 on v3

--- a/solution.py
+++ b/solution.py
@@ -181,11 +181,7 @@
 
     dense_all = lax.all_to_all(
         jnp.broadcast_to(dense_sum[None], (32, 32, 128)), PLANE, split_axis=0, concat_axis=0, tiled=True
-    ).reshape(1024, 128).astype(f32)
-    compress_grad = dense_all[:512].reshape(2, 256, 128)
-    expand_grad = dense_all[512:768].reshape(2, 128, 128)
-    gain_grad = dense_all[768:770] + dense_all[770:772]
-
+    ).reshape(1024, 128)
     other = swap_xl(table)
     pair = jnp.stack([jnp.where(low, table, other), jnp.where(low, other, table)])
     out = jnp.zeros((2, 8, R, 128), f32)
@@ -199,11 +195,17 @@
         up, down = shift_z(up, 1), shift_z(down, -1)
         out = put(out, up, z - step + 8)
         out = put(out, down, z + step)
+    up, down, dense_all = lax.optimization_barrier((up, down, dense_all))
     half_up = shift_z(up[:, :128], 1)
     half_down = shift_z(down[:, 128:], -1)
     out = put(out, half_up, z + 4)
     out = put(out, half_down, z + 4, 128)
     table_grad = out.reshape(16, R, 128)
+    dense_all = dense_all.astype(f32)
+    compress_grad = dense_all[:512].reshape(2, 256, 128)
+    expand_grad = dense_all[512:768].reshape(2, 128, 128)
+    gain_grad = dense_all[768:770] + dense_all[770:772]
+
     return (features_out, table_grad, compress_grad, expand_grad, gain_grad)
 
 

time: 146 us -> 144 us (0.986)
  waiting for transfers between devices: 59.7 us -> 58 us
    all_to_all x1, waiting for transfers between devices: 4.19 us -> 0.01 us  [on_device(): lax.all_to_all(jnp.broadcast_to(dense_sum[None], (32, 32, 128)), PLANE, s...]
    ppermute x8, waiting for transfers between devices: 5.41 us -> 7.87 us  [shift_z(): return lax.ppermute(x, 'z', [(i, (i + step) % 8) for i in range(8)])]
  transfers between devices with their start and end apart: 13 -> 13, of which waited for: 7 -> 7; matrix products, arithmetic and copies ran while one was open for 2% -> 1% of each run, Pallas kernels for 0% -> 0%
where the time goes in v4:
time: 144 us
  waiting for transfers between devices  58 us (40%)
  starting transfers between devices  32.7 us (23%)
  blocking collectives  27.2 us (19%)
  Pallas kernels  12.3 us (9%)
  local copies, waits for them, and re-layouts  6.3 us (4%)
  other arithmetic  4.04 us (3%)
  matrix products  2.27 us (2%)
    all_to_all x1, blocking collectives, on_device(): lax.all_to_all(table_part, 'z', split_axis=0, concat_axis=0, tiled=True)  27.2 us
    ppermute x2, waiting for transfers between devices, swap_xl(): return lax.ppermute(x, 'xl', [(0, 1), (1, 0)])  23.8 us
    all_to_all x1, waiting for transfers between devices, on_device(): lax.all_to_all(scaled, SHARD, split_axis=0, concat_axis=0, tiled=True)  23.3 us
    ppermute x8, starting transfers between devices, shift_z(): return lax.ppermute(x, 'z', [(i, (i + step) % 8) for i in range(8)])  13.2 us
    pallas_call x1, Pallas kernels, run_layers(): pl.pallas_call(layers_kernel, grid=(24 // B,), out_shape=(jax.ShapeDtypeS...  12.3 us
    ppermute x8, waiting for transfers between devices, shift_z(): return lax.ppermute(x, 'z', [(i, (i + step) % 8) for i in range(8)])  7.87 us
    all_to_all x1, starting transfers between devices, on_device(): lax.all_to_all(scaled, SHARD, split_axis=0, concat_axis=0, tiled=True)  6.27 us
    all_to_all x1, starting transfers between devices, on_device(): lax.all_to_all(jnp.broadcast_to(dense_sum[None], (32, 32, 128)), PLANE, s...  5.9 us
  transfers between devices with their start and end apart: 13, of which 7 were waited for; matrix products, arithmetic and copies ran while one was open for 1% of the time, Pallas kernels for 0%

profile of v4, /device:TPU:2, one launch (start us, length us, event | category | flops | bytes accessed | tf_op | source)
XLA Modules:
  0.0 143.7 jit_solution(6219463411554548811)
XLA Ops:
  0.6 0.0 copy-start
  0.6 0.9 copy.13
  1.5 3.0 %multiply_convert_fusion = bf16[384,16,128]{2,1,0:T(8,128)(2,1)} fusion(bf16[384,16,128]{2,1,0:T(8,128)(2,1)} %param.8, f32[384,16]{1,0:T(8,128)S(1)} %copy.13), kind=kLoop, calls=%fused_computation.7 | loop fusion | flops 2359296 | bytes 3170304 | tf_op jit(solution)/shard_map/convert_element_type | solution.py:155
  4.5 0.0 copy-start.7
  4.5 0.0 copy-start.2
  4.5 0.0 copy-start.3
  4.5 6.3 %all-to-all-start = ((bf16[384,16,128]{2,1,0:T(8,128)(2,1)}), bf16[384,16,128]{2,1,0:T(8,128)(2,1)S(1)}, u32[]{:S(2)}, u32[]{:S(2)}) async-start(bf16[384,16,128]{2,1,0:T(8,128)(2,1)} %multiply_convert_fusion), calls=%async_computation | async-start | bytes 3145728 | tf_op jit(solution)/shard_map/all_to_all | solution.py:157
  10.8 0.0 copy-done
  10.8 0.0 copy-done.7
  10.8 0.2 convolution_convert_fusion
  11.1 0.1 copy.16.w_ref
  11.2 23.3 %all-to-all-done = bf16[384,16,128]{2,1,0:T(8,128)(2,1)S(1)} async-done(((bf16[384,16,128]{2,1,0:T(8,128)(2,1)}), bf16[384,16,128]{2,1,0:T(8,128)(2,1)S(1)}, u32[]{:S(2)}, u32[]{:S(2)}) %all-to-all-start) | async-done | bytes 1572896 | tf_op jit(solution)/shard_map/all_to_all | solution.py:157
  34.6 0.0 copy-done.2
  34.6 0.0 copy-done.3
  34.6 0.0 copy-start.1
  34.6 1.4 copy-done.1
  36.0 12.3 %layers.1 = (bf16[24,256,128]{2,1,0:T(8,128)(2,1)}, bf16[32,224,128]{2,1,0:T(8,128)(2,1)}) custom-call(bf16[16,24,16,128]{3,2,1,0:T(8,128)(2,1)S(1)} %bitcast.87, bf16[24,256,128]{2,1,0:T(8,128)(2,1)S(1)} %copy-done.1, bf16[2,256,128]{2,1,0:T(8,128)(2,1)S(1)} %copy.16.w_ref, bf16[2,128,256]{2,1,0:T(8,128)(2,1)S(1)} %bitcast.89, ...), custom_call_target="tpu_custom_call" | custom-call | flops 4000000000 | bytes 7340032 | tf_op jit(solution)/shard_map/layers/pallas_call | solution.py:113
  48.3 0.0 copy-start.6
  48.3 0.0 copy-start.5
  48.3 5.3 %all-to-all-start.1 = ((bf16[32,224,128]{2,1,0:T(8,128)(2,1)}), bf16[32,224,128]{2,1,0:T(8,128)(2,1)S(1)}, u32[]{:S(2)}, u32[]{:S(2)}) async-start(bf16[32,224,128]{2,1,0:T(8,128)(2,1)} %get-tuple-element.11), calls=%async_computation.1 | async-start | bytes 3670016 | tf_op jit(solution)/shard_map/all_to_all | solution.py:166
  53.6 0.0 copy-done.6
  53.6 0.0 copy-done.5
  53.6 0.3 collective-permute-start
  54.0 21.2 %collective-permute-done = f32[2,8,384]{2,1,0:T(8,128)S(1)} collective-permute-done((f32[2,8,384]{2,1,0:T(8,128)S(1)}, f32[2,8,384]{2,1,0:T(8,128)S(1)}, u32[]{:S(2)}, u32[]{:S(2)}) %collective-permute-start) | collective-permute-done | bytes 24608 | tf_op jit(solution)/shard_map/ppermute | solution.py:146
  75.2 2.9 %all-to-all-done.1 = bf16[32,224,128]{2,1,0:T(8,128)(2,1)S(1)} async-done(((bf16[32,224,128]{2,1,0:T(8,128)(2,1)}), bf16[32,224,128]{2,1,0:T(8,128)(2,1)S(1)}, u32[]{:S(2)}, u32[]{:S(2)}) %all-to-all-start.1) | async-done | bytes 1835040 | tf_op jit(solution)/shard_map/all_to_all | solution.py:166
  78.2 0.2 slice.51
  78.3 1.0 fusion.2
  79.3 1.0 fusion.19
  80.4 0.1 slice_reduce_fusion
  80.5 27.2 %all_to_all.20 = bf16[8,288,128]{2,1,0:T(8,128)(2,1)S(1)} all-to-all(bf16[8,288,128]{2,1,0:T(8,128)(2,1)S(1)} %pad_maximum_fusion), channel_id=1, replica_groups=mesh['z'=8,'xl'=2,'y'=4,'xh'=2,'core'=2] {'z'}, dimensions={0} | all-to-all | bytes 1179648 | tf_op jit(solution)/shard_map/all_to_all | solution.py:178
  107.7 0.1 reduce_sum.25
  107.8 1.7 %collective-permute-start.1 = (bf16[256,128]{1,0:T(8,128)(2,1)S(1)}, bf16[256,128]{1,0:T(8,128)(2,1)S(1)}, u32[]{:S(2)}, u32[]{:S(2)}) collective-permute-start(bf16[256,128]{1,0:T(8,128)(2,1)S(1)} %slice.53), channel_id=1, source_target_pairs={{0,16},{16,0},{1,17},{17,1},{2,18},{18,2},{3,19},{19,3},{4,20},{20... | collective-permute-start | bytes 196616 | tf_op jit(solution)/shard_map/ppermute | solution.py:146
  109.5 2.6 %collective-permute-done.1 = bf16[256,128]{1,0:T(8,128)(2,1)S(1)} collective-permute-done((bf16[256,128]{1,0:T(8,128)(2,1)S(1)}, bf16[256,128]{1,0:T(8,128)(2,1)S(1)}, u32[]{:S(2)}, u32[]{:S(2)}) %collective-permute-start.1) | collective-permute-done | bytes 65568 | tf_op jit(solution)/shard_map/ppermute | solution.py:146
  112.2 0.6 collective-permute-start.2
  112.8 2.7 %collective-permute-start.3 = (bf16[2,256,128]{2,1,0:T(8,128)(2,1)S(1)}, bf16[2,256,128]{2,1,0:T(8,128)(2,1)S(1)}, u32[]{:S(2)}, u32[]{:S(2)}) collective-permute-start(bf16[2,256,128]{2,1,0:T(8,128)(2,1)S(1)} %pad_maximum_fusion.1), channel_id=1, source_target_pairs={{0,224},{32,0},{64,32},{96,64},{128,96},{160,128},{192,160},{224,1... | collective-permute-start | bytes 393224 | tf_op jit(solution)/shard_map/ppermute | solution.py:142
  115.5 0.7 broadcast_in_dim.105
  116.2 5.9 %all-to-all-start.3 = ((bf16[32,32,128]{2,1,0:T(8,128)(2,1)}), bf16[32,32,128]{2,1,0:T(8,128)(2,1)S(1)}, u32[]{:S(2)}, u32[]{:S(2)}) async-start(bf16[32,32,128]{2,1,0:T(8,128)(2,1)} %broadcast_in_dim.105), calls=%async_computation.3 | async-start | bytes 524288 | tf_op jit(solution)/shard_map/all_to_all | solution.py:182
  122.1 0.2 broadcast_in_dim.88
  122.4 0.0 collective-permute-done.2
  122.4 0.1 collective-permute-start.4
  122.5 0.0 collective-permute-done.3
  122.5 3.2 %collective-permute-start.5 = (bf16[2,256,128]{2,1,0:T(8,128)(2,1)S(1)}, bf16[2,256,128]{2,1,0:T(8,128)(2,1)S(1)}, u32[]{:S(2)}, u32[]{:S(2)}) collective-permute-start(bf16[2,256,128]{2,1,0:T(8,128)(2,1)S(1)} %collective-permute-done.3), channel_id=1, source_target_pairs={{0,224},{32,0},{64,32},{96,64},{128,96},{160,128},{192,160},{224,1... | collective-permute-start | bytes 393224 | tf_op jit(solution)/shard_map/ppermute | solution.py:142
  125.8 3.5 %collective-permute-done.4 = bf16[2,256,128]{2,1,0:T(8,128)(2,1)S(1)} collective-permute-done((bf16[2,256,128]{2,1,0:T(8,128)(2,1)S(1)}, bf16[2,256,128]{2,1,0:T(8,128)(2,1)S(1)}, u32[]{:S(2)}, u32[]{:S(2)}) %collective-permute-start.4) | collective-permute-done | bytes 131104 | tf_op jit(solution)/shard_map/ppermute | solution.py:142
  129.2 0.0 collective-permute-start.6
  129.2 0.0 collective-permute-done.5
  129.2 3.2 %collective-permute-start.7 = (bf16[2,256,128]{2,1,0:T(8,128)(2,1)S(1)}, bf16[2,256,128]{2,1,0:T(8,128)(2,1)S(1)}, u32[]{:S(2)}, u32[]{:S(2)}) collective-permute-start(bf16[2,256,128]{2,1,0:T(8,128)(2,1)S(1)} %collective-permute-done.5), channel_id=1, source_target_pairs={{0,224},{32,0},{64,32},{96,64},{128,96},{160,128},{192,160},{224,1... | collective-permute-start | bytes 393224 | tf_op jit(solution)/shard_map/ppermute | solution.py:142
  132.5 0.0 all-to-all-done.3
  132.5 2.9 %collective-permute-done.6 = bf16[2,256,128]{2,1,0:T(8,128)(2,1)S(1)} collective-permute-done((bf16[2,256,128]{2,1,0:T(8,128)(2,1)S(1)}, bf16[2,256,128]{2,1,0:T(8,128)(2,1)S(1)}, u32[]{:S(2)}, u32[]{:S(2)}) %collective-permute-start.6) | collective-permute-done | bytes 131104 | tf_op jit(solution)/shard_map/ppermute | solution.py:142
  135.4 0.0 collective-permute-done.7
  135.5 0.7 slice.55
  136.2 0.7 slice.56
  136.8 0.0 collective-permute-start.8
  136.9 3.3 %collective-permute-start.9 = (bf16[2,128,128]{2,1,0:T(8,128)(2,1)S(1)}, bf16[2,128,128]{2,1,0:T(8,128)(2,1)S(1)}, u32[]{:S(2)}, u32[]{:S(2)}) collective-permute-start(bf16[2,128,128]{2,1,0:T(8,128)(2,1)S(1)} %slice.44), channel_id=1, source_target_pairs={{0,224},{32,0},{64,32},{96,64},{128,96},{160,128},{192,160},{224,1... | collective-permute-start | bytes 196616 | tf_op jit(solution)/shard_map/ppermute | solution.py:142
  140.2 0.6 slice_add_fusion
  140.8 1.5 %collective-permute-done.8 = bf16[2,128,128]{2,1,0:T(8,128)(2,1)S(1)} collective-permute-done((bf16[2,128,128]{2,1,0:T(8,128)(2,1)S(1)}, bf16[2,128,128]{2,1,0:T(8,128)(2,1)S(1)}, u32[]{:S(2)}, u32[]{:S(2)}) %collective-permute-start.8) | collective-permute-done | bytes 65568 | tf_op jit(solution)/shard_map/ppermute | solution.py:142
  142.3 0.0 collective-permute-done.9
  142.4 0.0 copy-start.4
  142.4 1.3 copy-done.4
  (26 shorter events, 0.4 us)
Async XLA Ops:
  0.6 10.2 %copy-start = (bf16[2,256,128]{2,1,0:T(8,128)(2,1)S(1)}, bf16[2,256,128]{2,1,0:T(8,128)(2,1)}, u32[]{:S(2)}) copy-start(bf16[2,256,128]{2,1,0:T(8,128)(2,1)} %param.12) | copy-start | bytes 393220
  4.5 6.3 %copy-start.7 = (s32[256]{0:T(256)S(1)}, s32[256]{0:T(256)}, u32[]{:S(2)}) copy-start(s32[256]{0:T(256)} %param.11) | copy-start | bytes 3076
  4.5 30.0 %copy-start.2 = (bf16[2,128,128]{2,1,0:T(8,128)(2,1)S(1)}, bf16[2,128,128]{2,1,0:T(8,128)(2,1)}, u32[]{:S(2)}) copy-start(bf16[2,128,128]{2,1,0:T(8,128)(2,1)} %v_ref.1) | copy-start | bytes 196612
  4.5 30.0 %copy-start.3 = (f32[2,128]{1,0:T(2,128)S(1)}, f32[2,128]{1,0:T(2,128)}, u32[]{:S(2)}) copy-start(f32[2,128]{1,0:T(2,128)} %gain_ref.1) | copy-start | bytes 3076
  4.5 30.0 %all-to-all-start = ((bf16[384,16,128]{2,1,0:T(8,128)(2,1)}), bf16[384,16,128]{2,1,0:T(8,128)(2,1)S(1)}, u32[]{:S(2)}, u32[]{:S(2)}) async-start(bf16[384,16,128]{2,1,0:T(8,128)(2,1)} %multiply_convert_fusion), calls=%async_computation | async-start | bytes 3145728 | tf_op jit(solution)/shard_map/all_to_all | solution.py:157
  34.6 1.4 copy-start.1
  48.3 5.3 %copy-start.6 = (s32[384,16]{0,1:T(8,128)S(1)}, s32[384,16]{0,1:T(8,128)}, u32[]{:S(2)}) copy-start(s32[384,16]{0,1:T(8,128)} %param.10) | copy-start | bytes 73732
  48.3 5.3 %copy-start.5 = (f32[384,16]{0,1:T(8,128)S(1)}, f32[384,16]{0,1:T(8,128)}, u32[]{:S(2)}) copy-start(f32[384,16]{0,1:T(8,128)} %param.9) | copy-start | bytes 73732
  48.3 29.8 %all-to-all-start.1 = ((bf16[32,224,128]{2,1,0:T(8,128)(2,1)}), bf16[32,224,128]{2,1,0:T(8,128)(2,1)S(1)}, u32[]{:S(2)}, u32[]{:S(2)}) async-start(bf16[32,224,128]{2,1,0:T(8,128)(2,1)} %get-tuple-element.11), calls=%async_computation.1 | async-start | bytes 3670016 | tf_op jit(solution)/shard_map/all_to_all | solution.py:166
  53.6 21.5 %collective-permute-start = (f32[2,8,384]{2,1,0:T(8,128)S(1)}, f32[2,8,384]{2,1,0:T(8,128)S(1)}, u32[]{:S(2)}, u32[]{:S(2)}) collective-permute-start(f32[2,8,384]{2,1,0:T(8,128)S(1)} %dynamic-slice_bitcast_fusion), channel_id=1, source_target_pairs={{0,16},{16,0},{1,17},{17,1},{2,18},{18,2},{3,19},{19,3},{4,20},{20... | collective-permute-start | bytes 73736 | tf_op jit(solution)/shard_map/ppermute | solution.py:146
  107.8 4.4 %collective-permute-start.1 = (bf16[256,128]{1,0:T(8,128)(2,1)S(1)}, bf16[256,128]{1,0:T(8,128)(2,1)S(1)}, u32[]{:S(2)}, u32[]{:S(2)}) collective-permute-start(bf16[256,128]{1,0:T(8,128)(2,1)S(1)} %slice.53), channel_id=1, source_target_pairs={{0,16},{16,0},{1,17},{17,1},{2,18},{18,2},{3,19},{19,3},{4,20},{20... | collective-permute-start | bytes 196616 | tf_op jit(solution)/shard_map/ppermute | solution.py:146
  112.2 10.2 %collective-permute-start.2 = (bf16[2,256,128]{2,1,0:T(8,128)(2,1)S(1)}, bf16[2,256,128]{2,1,0:T(8,128)(2,1)S(1)}, u32[]{:S(2)}, u32[]{:S(2)}) collective-permute-start(bf16[2,256,128]{2,1,0:T(8,128)(2,1)S(1)} %pad_maximum_fusion.1), channel_id=1, source_target_pairs={{0,32},{32,64},{64,96},{96,128},{128,160},{160,192},{192,224},{224... | collective-permute-start | bytes 393224 | tf_op jit(solution)/shard_map/ppermute | solution.py:142
  112.8 9.7 %collective-permute-start.3 = (bf16[2,256,128]{2,1,0:T(8,128)(2,1)S(1)}, bf16[2,256,128]{2,1,0:T(8,128)(2,1)S(1)}, u32[]{:S(2)}, u32[]{:S(2)}) collective-permute-start(bf16[2,256,128]{2,1,0:T(8,128)(2,1)S(1)} %pad_maximum_fusion.1), channel_id=1, source_target_pairs={{0,224},{32,0},{64,32},{96,64},{128,96},{160,128},{192,160},{224,1... | collective-permute-start | bytes 393224 | tf_op jit(solution)/shard_map/ppermute | solution.py:142
  116.2 16.3 %all-to-all-start.3 = ((bf16[32,32,128]{2,1,0:T(8,128)(2,1)}), bf16[32,32,128]{2,1,0:T(8,128)(2,1)S(1)}, u32[]{:S(2)}, u32[]{:S(2)}) async-start(bf16[32,32,128]{2,1,0:T(8,128)(2,1)} %broadcast_in_dim.105), calls=%async_computation.3 | async-start | bytes 524288 | tf_op jit(solution)/shard_map/all_to_all | solution.py:182
  122.4 6.8 %collective-permute-start.4 = (bf16[2,256,128]{2,1,0:T(8,128)(2,1)S(1)}, bf16[2,256,128]{2,1,0:T(8,128)(2,1)S(1)}, u32[]{:S(2)}, u32[]{:S(2)}) collective-permute-start(bf16[2,256,128]{2,1,0:T(8,128)(2,1)S(1)} %collective-permute-done.2), channel_id=1, source_target_pairs={{0,32},{32,64},{64,96},{96,128},{128,160},{160,192},{192,224},{224... | collective-permute-start | bytes 393224 | tf_op jit(solution)/shard_map/ppermute | solution.py:142
  122.5 6.7 %collective-permute-start.5 = (bf16[2,256,128]{2,1,0:T(8,128)(2,1)S(1)}, bf16[2,256,128]{2,1,0:T(8,128)(2,1)S(1)}, u32[]{:S(2)}, u32[]{:S(2)}) collective-permute-start(bf16[2,256,128]{2,1,0:T(8,128)(2,1)S(1)} %collective-permute-done.3), channel_id=1, source_target_pairs={{0,224},{32,0},{64,32},{96,64},{128,96},{160,128},{192,160},{224,1... | collective-permute-start | bytes 393224 | tf_op jit(solution)/shard_map/ppermute | solution.py:142
  129.2 6.2 %collective-permute-start.6 = (bf16[2,256,128]{2,1,0:T(8,128)(2,1)S(1)}, bf16[2,256,128]{2,1,0:T(8,128)(2,1)S(1)}, u32[]{:S(2)}, u32[]{:S(2)}) collective-permute-start(bf16[2,256,128]{2,1,0:T(8,128)(2,1)S(1)} %collective-permute-done.4), channel_id=1, source_target_pairs={{0,32},{32,64},{64,96},{96,128},{128,160},{160,192},{192,224},{224... | collective-permute-start | bytes 393224 | tf_op jit(solution)/shard_map/ppermute | solution.py:142
  129.2 6.2 %collective-permute-start.7 = (bf16[2,256,128]{2,1,0:T(8,128)(2,1)S(1)}, bf16[2,256,128]{2,1,0:T(8,128)(2,1)S(1)}, u32[]{:S(2)}, u32[]{:S(2)}) collective-permute-start(bf16[2,256,128]{2,1,0:T(8,128)(2,1)S(1)} %collective-permute-done.5), channel_id=1, source_target_pairs={{0,224},{32,0},{64,32},{96,64},{128,96},{160,128},{192,160},{224,1... | collective-permute-start | bytes 393224 | tf_op jit(solution)/shard_map/ppermute | solution.py:142
  136.8 5.5 %collective-permute-start.8 = (bf16[2,128,128]{2,1,0:T(8,128)(2,1)S(1)}, bf16[2,128,128]{2,1,0:T(8,128)(2,1)S(1)}, u32[]{:S(2)}, u32[]{:S(2)}) collective-permute-start(bf16[2,128,128]{2,1,0:T(8,128)(2,1)S(1)} %slice.43), channel_id=1, source_target_pairs={{0,32},{32,64},{64,96},{96,128},{128,160},{160,192},{192,224},{224... | collective-permute-start | bytes 196616 | tf_op jit(solution)/shard_map/ppermute | solution.py:142
  136.9 5.5 %collective-permute-start.9 = (bf16[2,128,128]{2,1,0:T(8,128)(2,1)S(1)}, bf16[2,128,128]{2,1,0:T(8,128)(2,1)S(1)}, u32[]{:S(2)}, u32[]{:S(2)}) collective-permute-start(bf16[2,128,128]{2,1,0:T(8,128)(2,1)S(1)} %slice.44), channel_id=1, source_target_pairs={{0,224},{32,0},{64,32},{96,64},{128,96},{160,128},{192,160},{224,1... | collective-permute-start | bytes 196616 | tf_op jit(solution)/shard_map/ppermute | solution.py:142
  142.4 1.3 copy-start.4

commit v5 on v4

--- a/solution.py
+++ b/solution.py
@@ -18,7 +18,7 @@
 
 NT = ((1,), (1,))
 TN = ((0,), (0,))
-B = 12
+B = 24
 G = 6
 
 
@@ -179,10 +179,10 @@
     summed = jnp.sum(table_part.astype(f32), axis=0).astype(bf16)
     table, dense_sum = summed[:256], summed[256:]
 
-    dense_all = lax.all_to_all(
-        jnp.broadcast_to(dense_sum[None], (32, 32, 128)), PLANE, split_axis=0, concat_axis=0, tiled=True
-    ).reshape(1024, 128)
+    copies = jnp.broadcast_to(dense_sum[None], (32, 32, 128))
     other = swap_xl(table)
+    copies, other = lax.optimization_barrier((copies, other))
+    dense_all = lax.all_to_all(copies, PLANE, split_axis=0, concat_axis=0, tiled=True).reshape(1024, 128)
     pair = jnp.stack([jnp.where(low, table, other), jnp.where(low, other, table)])
     out = jnp.zeros((2, 8, R, 128), f32)
 

time: 144 us -> 144 us (level)
  no operation moved by 1% of the time
where the time goes in v5:
time: 144 us; the launch traced here: 143 us
  waiting for transfers between devices  57.8 us (40%)
  starting transfers between devices  32.8 us (23%)
  blocking collectives  27.2 us (19%)
  Pallas kernels  11.9 us (8%)
  local copies, waits for them, and re-layouts  6.3 us (4%)
  other arithmetic  4.04 us (3%)
  matrix products  2.27 us (2%)
    all_to_all x1, blocking collectives, on_device(): lax.all_to_all(table_part, 'z', split_axis=0, concat_axis=0, tiled=True)  27.2 us
    ppermute x2, waiting for transfers between devices, swap_xl(): return lax.ppermute(x, 'xl', [(0, 1), (1, 0)])  23.6 us
    all_to_all x1, waiting for transfers between devices, on_device(): lax.all_to_all(scaled, SHARD, split_axis=0, concat_axis=0, tiled=True)  23.3 us
    ppermute x8, starting transfers between devices, shift_z(): return lax.ppermute(x, 'z', [(i, (i + step) % 8) for i in range(8)])  13.2 us
    pallas_call x1, Pallas kernels, run_layers(): pl.pallas_call(layers_kernel, grid=(24 // B,), out_shape=(jax.ShapeDtypeS...  11.9 us
    ppermute x8, waiting for transfers between devices, shift_z(): return lax.ppermute(x, 'z', [(i, (i + step) % 8) for i in range(8)])  7.87 us
    all_to_all x1, starting transfers between devices, on_device(): lax.all_to_all(scaled, SHARD, split_axis=0, concat_axis=0, tiled=True)  6.27 us
    all_to_all x1, starting transfers between devices, on_device(): lax.all_to_all(copies, PLANE, split_axis=0, concat_axis=0, tiled=True)  5.9 us
  transfers between devices with their start and end apart: 13, of which 7 were waited for; matrix products, arithmetic and copies ran while one was open for 1% of the time, Pallas kernels for 0%

profile of v5, /device:TPU:2, one launch (start us, length us, event | category | flops | bytes accessed | tf_op | source)
XLA Modules:
  0.0 143.2 jit_solution(14303741522430326746)
XLA Ops:
  0.6 0.0 copy-start
  0.6 0.9 copy.13
  1.5 3.0 %multiply_convert_fusion = bf16[384,16,128]{2,1,0:T(8,128)(2,1)} fusion(bf16[384,16,128]{2,1,0:T(8,128)(2,1)} %param.8, f32[384,16]{1,0:T(8,128)S(1)} %copy.13), kind=kLoop, calls=%fused_computation.7 | loop fusion | flops 2359296 | bytes 3170304 | tf_op jit(solution)/shard_map/convert_element_type | solution.py:155
  4.5 0.0 copy-start.7
  4.5 0.0 copy-start.2
  4.5 0.0 copy-start.3
  4.5 6.3 %all-to-all-start = ((bf16[384,16,128]{2,1,0:T(8,128)(2,1)}), bf16[384,16,128]{2,1,0:T(8,128)(2,1)S(1)}, u32[]{:S(2)}, u32[]{:S(2)}) async-start(bf16[384,16,128]{2,1,0:T(8,128)(2,1)} %multiply_convert_fusion), calls=%async_computation | async-start | bytes 3145728 | tf_op jit(solution)/shard_map/all_to_all | solution.py:157
  10.8 0.0 copy-done
  10.8 0.0 copy-done.7
  10.8 0.2 convolution_convert_fusion
  11.1 0.1 copy.16.w_ref
  11.2 23.3 %all-to-all-done = bf16[384,16,128]{2,1,0:T(8,128)(2,1)S(1)} async-done(((bf16[384,16,128]{2,1,0:T(8,128)(2,1)}), bf16[384,16,128]{2,1,0:T(8,128)(2,1)S(1)}, u32[]{:S(2)}, u32[]{:S(2)}) %all-to-all-start) | async-done | bytes 1572896 | tf_op jit(solution)/shard_map/all_to_all | solution.py:157
  34.6 0.0 copy-done.2
  34.6 0.0 copy-done.3
  34.6 0.0 copy-start.1
  34.6 1.4 copy-done.1
  36.0 11.9 %layers.1 = (bf16[24,256,128]{2,1,0:T(8,128)(2,1)}, bf16[32,224,128]{2,1,0:T(8,128)(2,1)}) custom-call(bf16[16,24,16,128]{3,2,1,0:T(8,128)(2,1)S(1)} %bitcast.87, bf16[24,256,128]{2,1,0:T(8,128)(2,1)S(1)} %copy-done.1, bf16[2,256,128]{2,1,0:T(8,128)(2,1)S(1)} %copy.16.w_ref, bf16[2,128,256]{2,1,0:T(8,128)(2,1)S(1)} %bitcast.89, ...), custom_call_target="tpu_custom_call" | custom-call | flops 4000000000 | bytes 7340032 | tf_op jit(solution)/shard_map/layers/pallas_call | solution.py:113
  47.9 0.0 copy-start.6
  47.9 0.0 copy-start.5
  47.9 5.2 %all-to-all-start.1 = ((bf16[32,224,128]{2,1,0:T(8,128)(2,1)}), bf16[32,224,128]{2,1,0:T(8,128)(2,1)S(1)}, u32[]{:S(2)}, u32[]{:S(2)}) async-start(bf16[32,224,128]{2,1,0:T(8,128)(2,1)} %get-tuple-element.13), calls=%async_computation.1 | async-start | bytes 3670016 | tf_op jit(solution)/shard_map/all_to_all | solution.py:166
  53.1 0.0 copy-done.6
  53.1 0.0 copy-done.5
  53.2 0.5 collective-permute-start
  53.7 21.0 %collective-permute-done = f32[2,8,384]{2,1,0:T(8,128)S(1)} collective-permute-done((f32[2,8,384]{2,1,0:T(8,128)S(1)}, f32[2,8,384]{2,1,0:T(8,128)S(1)}, u32[]{:S(2)}, u32[]{:S(2)}) %collective-permute-start) | collective-permute-done | bytes 24608 | tf_op jit(solution)/shard_map/ppermute | solution.py:146
  74.7 2.9 %all-to-all-done.1 = bf16[32,224,128]{2,1,0:T(8,128)(2,1)S(1)} async-done(((bf16[32,224,128]{2,1,0:T(8,128)(2,1)}), bf16[32,224,128]{2,1,0:T(8,128)(2,1)S(1)}, u32[]{:S(2)}, u32[]{:S(2)}) %all-to-all-start.1) | async-done | bytes 1835040 | tf_op jit(solution)/shard_map/all_to_all | solution.py:166
  77.7 0.2 slice.51
  77.9 1.0 fusion.2
  78.9 1.0 fusion.19
  79.9 0.1 slice_reduce_fusion
  80.0 27.2 %all_to_all.20 = bf16[8,288,128]{2,1,0:T(8,128)(2,1)S(1)} all-to-all(bf16[8,288,128]{2,1,0:T(8,128)(2,1)S(1)} %pad_maximum_fusion), channel_id=1, replica_groups=mesh['z'=8,'xl'=2,'y'=4,'xh'=2,'core'=2] {'z'}, dimensions={0} | all-to-all | bytes 1179648 | tf_op jit(solution)/shard_map/all_to_all | solution.py:178
  107.2 0.1 reduce_sum.25
  107.3 1.7 %collective-permute-start.1 = (bf16[256,128]{1,0:T(8,128)(2,1)S(1)}, bf16[256,128]{1,0:T(8,128)(2,1)S(1)}, u32[]{:S(2)}, u32[]{:S(2)}) collective-permute-start(bf16[256,128]{1,0:T(8,128)(2,1)S(1)} %slice.53), channel_id=1, source_target_pairs={{0,16},{16,0},{1,17},{17,1},{2,18},{18,2},{3,19},{19,3},{4,20},{20... | collective-permute-start | bytes 196616 | tf_op jit(solution)/shard_map/ppermute | solution.py:146
  109.1 2.6 %collective-permute-done.1 = bf16[256,128]{1,0:T(8,128)(2,1)S(1)} collective-permute-done((bf16[256,128]{1,0:T(8,128)(2,1)S(1)}, bf16[256,128]{1,0:T(8,128)(2,1)S(1)}, u32[]{:S(2)}, u32[]{:S(2)}) %collective-permute-start.1) | collective-permute-done | bytes 65568 | tf_op jit(solution)/shard_map/ppermute | solution.py:146
  111.7 0.7 broadcast_in_dim.93
  112.5 0.6 collective-permute-start.2
  113.1 2.7 %collective-permute-start.3 = (bf16[2,256,128]{2,1,0:T(8,128)(2,1)S(1)}, bf16[2,256,128]{2,1,0:T(8,128)(2,1)S(1)}, u32[]{:S(2)}, u32[]{:S(2)}) collective-permute-start(bf16[2,256,128]{2,1,0:T(8,128)(2,1)S(1)} %pad_maximum_fusion.1), channel_id=1, source_target_pairs={{0,224},{32,0},{64,32},{96,64},{128,96},{160,128},{192,160},{224,1... | collective-permute-start | bytes 393224 | tf_op jit(solution)/shard_map/ppermute | solution.py:142
  115.8 5.9 %all-to-all-start.3 = ((bf16[32,32,128]{2,1,0:T(8,128)(2,1)}), bf16[32,32,128]{2,1,0:T(8,128)(2,1)S(1)}, u32[]{:S(2)}, u32[]{:S(2)}) async-start(bf16[32,32,128]{2,1,0:T(8,128)(2,1)} %broadcast_in_dim.93), calls=%async_computation.3 | async-start | bytes 524288 | tf_op jit(solution)/shard_map/all_to_all | solution.py:185
  121.7 0.2 broadcast_in_dim.88
  121.9 0.0 collective-permute-done.2
  121.9 0.1 collective-permute-start.4
  122.0 0.0 collective-permute-done.3
  122.0 3.2 %collective-permute-start.5 = (bf16[2,256,128]{2,1,0:T(8,128)(2,1)S(1)}, bf16[2,256,128]{2,1,0:T(8,128)(2,1)S(1)}, u32[]{:S(2)}, u32[]{:S(2)}) collective-permute-start(bf16[2,256,128]{2,1,0:T(8,128)(2,1)S(1)} %collective-permute-done.3), channel_id=1, source_target_pairs={{0,224},{32,0},{64,32},{96,64},{128,96},{160,128},{192,160},{224,1... | collective-permute-start | bytes 393224 | tf_op jit(solution)/shard_map/ppermute | solution.py:142
  125.3 3.5 %collective-permute-done.4 = bf16[2,256,128]{2,1,0:T(8,128)(2,1)S(1)} collective-permute-done((bf16[2,256,128]{2,1,0:T(8,128)(2,1)S(1)}, bf16[2,256,128]{2,1,0:T(8,128)(2,1)S(1)}, u32[]{:S(2)}, u32[]{:S(2)}) %collective-permute-start.4) | collective-permute-done | bytes 131104 | tf_op jit(solution)/shard_map/ppermute | solution.py:142
  128.8 0.0 collective-permute-start.6
  128.8 0.0 collective-permute-done.5
  128.8 3.2 %collective-permute-start.7 = (bf16[2,256,128]{2,1,0:T(8,128)(2,1)S(1)}, bf16[2,256,128]{2,1,0:T(8,128)(2,1)S(1)}, u32[]{:S(2)}, u32[]{:S(2)}) collective-permute-start(bf16[2,256,128]{2,1,0:T(8,128)(2,1)S(1)} %collective-permute-done.5), channel_id=1, source_target_pairs={{0,224},{32,0},{64,32},{96,64},{128,96},{160,128},{192,160},{224,1... | collective-permute-start | bytes 393224 | tf_op jit(solution)/shard_map/ppermute | solution.py:142
  132.1 0.0 all-to-all-done.3
  132.1 2.9 %collective-permute-done.6 = bf16[2,256,128]{2,1,0:T(8,128)(2,1)S(1)} collective-permute-done((bf16[2,256,128]{2,1,0:T(8,128)(2,1)S(1)}, bf16[2,256,128]{2,1,0:T(8,128)(2,1)S(1)}, u32[]{:S(2)}, u32[]{:S(2)}) %collective-permute-start.6) | collective-permute-done | bytes 131104 | tf_op jit(solution)/shard_map/ppermute | solution.py:142
  135.0 0.0 collective-permute-done.7
  135.0 0.7 slice.55
  135.7 0.7 slice.56
  136.4 0.0 collective-permute-start.8
  136.4 3.3 %collective-permute-start.9 = (bf16[2,128,128]{2,1,0:T(8,128)(2,1)S(1)}, bf16[2,128,128]{2,1,0:T(8,128)(2,1)S(1)}, u32[]{:S(2)}, u32[]{:S(2)}) collective-permute-start(bf16[2,128,128]{2,1,0:T(8,128)(2,1)S(1)} %slice.44), channel_id=1, source_target_pairs={{0,224},{32,0},{64,32},{96,64},{128,96},{160,128},{192,160},{224,1... | collective-permute-start | bytes 196616 | tf_op jit(solution)/shard_map/ppermute | solution.py:142
  139.7 0.6 slice_add_fusion
  140.4 1.5 %collective-permute-done.8 = bf16[2,128,128]{2,1,0:T(8,128)(2,1)S(1)} collective-permute-done((bf16[2,128,128]{2,1,0:T(8,128)(2,1)S(1)}, bf16[2,128,128]{2,1,0:T(8,128)(2,1)S(1)}, u32[]{:S(2)}, u32[]{:S(2)}) %collective-permute-start.8) | collective-permute-done | bytes 65568 | tf_op jit(solution)/shard_map/ppermute | solution.py:142
  141.9 0.0 collective-permute-done.9
  141.9 0.0 copy-start.4
  141.9 1.3 copy-done.4
  (26 shorter events, 0.4 us)
Async XLA Ops:
  0.6 10.2 %copy-start = (bf16[2,256,128]{2,1,0:T(8,128)(2,1)S(1)}, bf16[2,256,128]{2,1,0:T(8,128)(2,1)}, u32[]{:S(2)}) copy-start(bf16[2,256,128]{2,1,0:T(8,128)(2,1)} %param.12) | copy-start | bytes 393220
  4.5 6.3 %copy-start.7 = (s32[256]{0:T(256)S(1)}, s32[256]{0:T(256)}, u32[]{:S(2)}) copy-start(s32[256]{0:T(256)} %param.11) | copy-start | bytes 3076
  4.5 30.0 %copy-start.2 = (bf16[2,128,128]{2,1,0:T(8,128)(2,1)S(1)}, bf16[2,128,128]{2,1,0:T(8,128)(2,1)}, u32[]{:S(2)}) copy-start(bf16[2,128,128]{2,1,0:T(8,128)(2,1)} %v_ref.1) | copy-start | bytes 196612
  4.5 30.0 %copy-start.3 = (f32[2,128]{1,0:T(2,128)S(1)}, f32[2,128]{1,0:T(2,128)}, u32[]{:S(2)}) copy-start(f32[2,128]{1,0:T(2,128)} %gain_ref.1) | copy-start | bytes 3076
  4.5 30.0 %all-to-all-start = ((bf16[384,16,128]{2,1,0:T(8,128)(2,1)}), bf16[384,16,128]{2,1,0:T(8,128)(2,1)S(1)}, u32[]{:S(2)}, u32[]{:S(2)}) async-start(bf16[384,16,128]{2,1,0:T(8,128)(2,1)} %multiply_convert_fusion), calls=%async_computation | async-start | bytes 3145728 | tf_op jit(solution)/shard_map/all_to_all | solution.py:157
  34.6 1.4 copy-start.1
  47.9 5.3 %copy-start.6 = (s32[384,16]{0,1:T(8,128)S(1)}, s32[384,16]{0,1:T(8,128)}, u32[]{:S(2)}) copy-start(s32[384,16]{0,1:T(8,128)} %param.10) | copy-start | bytes 73732
  47.9 5.3 %copy-start.5 = (f32[384,16]{0,1:T(8,128)S(1)}, f32[384,16]{0,1:T(8,128)}, u32[]{:S(2)}) copy-start(f32[384,16]{0,1:T(8,128)} %param.9) | copy-start | bytes 73732
  47.9 29.8 %all-to-all-start.1 = ((bf16[32,224,128]{2,1,0:T(8,128)(2,1)}), bf16[32,224,128]{2,1,0:T(8,128)(2,1)S(1)}, u32[]{:S(2)}, u32[]{:S(2)}) async-start(bf16[32,224,128]{2,1,0:T(8,128)(2,1)} %get-tuple-element.13), calls=%async_computation.1 | async-start | bytes 3670016 | tf_op jit(solution)/shard_map/all_to_all | solution.py:166
  53.2 21.5 %collective-permute-start = (f32[2,8,384]{2,1,0:T(8,128)S(1)}, f32[2,8,384]{2,1,0:T(8,128)S(1)}, u32[]{:S(2)}, u32[]{:S(2)}) collective-permute-start(f32[2,8,384]{2,1,0:T(8,128)S(1)} %dynamic-slice_bitcast_fusion), channel_id=1, source_target_pairs={{0,16},{16,0},{1,17},{17,1},{2,18},{18,2},{3,19},{19,3},{4,20},{20... | collective-permute-start | bytes 73736 | tf_op jit(solution)/shard_map/ppermute | solution.py:146
  107.3 4.4 %collective-permute-start.1 = (bf16[256,128]{1,0:T(8,128)(2,1)S(1)}, bf16[256,128]{1,0:T(8,128)(2,1)S(1)}, u32[]{:S(2)}, u32[]{:S(2)}) collective-permute-start(bf16[256,128]{1,0:T(8,128)(2,1)S(1)} %slice.53), channel_id=1, source_target_pairs={{0,16},{16,0},{1,17},{17,1},{2,18},{18,2},{3,19},{19,3},{4,20},{20... | collective-permute-start | bytes 196616 | tf_op jit(solution)/shard_map/ppermute | solution.py:146
  112.5 9.5 %collective-permute-start.2 = (bf16[2,256,128]{2,1,0:T(8,128)(2,1)S(1)}, bf16[2,256,128]{2,1,0:T(8,128)(2,1)S(1)}, u32[]{:S(2)}, u32[]{:S(2)}) collective-permute-start(bf16[2,256,128]{2,1,0:T(8,128)(2,1)S(1)} %pad_maximum_fusion.1), channel_id=1, source_target_pairs={{0,32},{32,64},{64,96},{96,128},{128,160},{160,192},{192,224},{224... | collective-permute-start | bytes 393224 | tf_op jit(solution)/shard_map/ppermute | solution.py:142
  113.1 8.9 %collective-permute-start.3 = (bf16[2,256,128]{2,1,0:T(8,128)(2,1)S(1)}, bf16[2,256,128]{2,1,0:T(8,128)(2,1)S(1)}, u32[]{:S(2)}, u32[]{:S(2)}) collective-permute-start(bf16[2,256,128]{2,1,0:T(8,128)(2,1)S(1)} %pad_maximum_fusion.1), channel_id=1, source_target_pairs={{0,224},{32,0},{64,32},{96,64},{128,96},{160,128},{192,160},{224,1... | collective-permute-start | bytes 393224 | tf_op jit(solution)/shard_map/ppermute | solution.py:142
  115.8 16.3 %all-to-all-start.3 = ((bf16[32,32,128]{2,1,0:T(8,128)(2,1)}), bf16[32,32,128]{2,1,0:T(8,128)(2,1)S(1)}, u32[]{:S(2)}, u32[]{:S(2)}) async-start(bf16[32,32,128]{2,1,0:T(8,128)(2,1)} %broadcast_in_dim.93), calls=%async_computation.3 | async-start | bytes 524288 | tf_op jit(solution)/shard_map/all_to_all | solution.py:185
  121.9 6.8 %collective-permute-start.4 = (bf16[2,256,128]{2,1,0:T(8,128)(2,1)S(1)}, bf16[2,256,128]{2,1,0:T(8,128)(2,1)S(1)}, u32[]{:S(2)}, u32[]{:S(2)}) collective-permute-start(bf16[2,256,128]{2,1,0:T(8,128)(2,1)S(1)} %collective-permute-done.2), channel_id=1, source_target_pairs={{0,32},{32,64},{64,96},{96,128},{128,160},{160,192},{192,224},{224... | collective-permute-start | bytes 393224 | tf_op jit(solution)/shard_map/ppermute | solution.py:142
  122.0 6.7 %collective-permute-start.5 = (bf16[2,256,128]{2,1,0:T(8,128)(2,1)S(1)}, bf16[2,256,128]{2,1,0:T(8,128)(2,1)S(1)}, u32[]{:S(2)}, u32[]{:S(2)}) collective-permute-start(bf16[2,256,128]{2,1,0:T(8,128)(2,1)S(1)} %collective-permute-done.3), channel_id=1, source_target_pairs={{0,224},{32,0},{64,32},{96,64},{128,96},{160,128},{192,160},{224,1... | collective-permute-start | bytes 393224 | tf_op jit(solution)/shard_map/ppermute | solution.py:142
  128.8 6.2 %collective-permute-start.6 = (bf16[2,256,128]{2,1,0:T(8,128)(2,1)S(1)}, bf16[2,256,128]{2,1,0:T(8,128)(2,1)S(1)}, u32[]{:S(2)}, u32[]{:S(2)}) collective-permute-start(bf16[2,256,128]{2,1,0:T(8,128)(2,1)S(1)} %collective-permute-done.4), channel_id=1, source_target_pairs={{0,32},{32,64},{64,96},{96,128},{128,160},{160,192},{192,224},{224... | collective-permute-start | bytes 393224 | tf_op jit(solution)/shard_map/ppermute | solution.py:142
  128.8 6.2 %collective-permute-start.7 = (bf16[2,256,128]{2,1,0:T(8,128)(2,1)S(1)}, bf16[2,256,128]{2,1,0:T(8,128)(2,1)S(1)}, u32[]{:S(2)}, u32[]{:S(2)}) collective-permute-start(bf16[2,256,128]{2,1,0:T(8,128)(2,1)S(1)} %collective-permute-done.5), channel_id=1, source_target_pairs={{0,224},{32,0},{64,32},{96,64},{128,96},{160,128},{192,160},{224,1... | collective-permute-start | bytes 393224 | tf_op jit(solution)/shard_map/ppermute | solution.py:142
  136.4 5.5 %collective-permute-start.8 = (bf16[2,128,128]{2,1,0:T(8,128)(2,1)S(1)}, bf16[2,128,128]{2,1,0:T(8,128)(2,1)S(1)}, u32[]{:S(2)}, u32[]{:S(2)}) collective-permute-start(bf16[2,128,128]{2,1,0:T(8,128)(2,1)S(1)} %slice.43), channel_id=1, source_target_pairs={{0,32},{32,64},{64,96},{96,128},{128,160},{160,192},{192,224},{224... | collective-permute-start | bytes 196616 | tf_op jit(solution)/shard_map/ppermute | solution.py:142
  136.4 5.5 %collective-permute-start.9 = (bf16[2,128,128]{2,1,0:T(8,128)(2,1)S(1)}, bf16[2,128,128]{2,1,0:T(8,128)(2,1)S(1)}, u32[]{:S(2)}, u32[]{:S(2)}) collective-permute-start(bf16[2,128,128]{2,1,0:T(8,128)(2,1)S(1)} %slice.44), channel_id=1, source_target_pairs={{0,224},{32,0},{64,32},{96,64},{128,96},{160,128},{192,160},{224,1... | collective-permute-start | bytes 196616 | tf_op jit(solution)/shard_map/ppermute | solution.py:142
  141.9 1.3 copy-start.4
